TPU v7x, 128 devices: a whole 4x4x4 slice. The times are simulated.
128 devices in a mesh: dp: 4 (over y), expert: 32 (over x, z, core).
Axes of the slice: x: 4, y: 4, z: 4, core: 2. Of those that a mesh axis runs over, the one named last changes fastest.
Arguments:
- out_grad: bfloat16 [16384, 2880], P(('dp', 'expert')), may hold values from -6 to 6
- expert_ids: int32 [16384, 4], P(('dp', 'expert')), may hold values from 0 to 31, all different within a row; in each aligned block of 128 rows (0 to 127, 128 to 255, ...) at most 20 rows name the same one
- chosen_logits: float32 [16384, 4], P(('dp', 'expert')), may hold values from -6 to 6
- router_weight: bfloat16 [2880, 32], replicated, may hold values from -2 to 2
- hidden_act: bfloat16 [32, 128, 20, 2880], P('expert', None, None, 'dp'), may hold values from -0.29882812 to 0.29882812
- down_weight: bfloat16 [32, 2880, 2880], P('expert', 'dp'), may hold values from -0.109375 to 0.109375
- attn_out: bfloat16 [16384, 2048], P(('dp', 'expert')), may hold values from -6 to 6
- proj_weight: bfloat16 [2048, 2880], P('dp'), may hold values from -0.125 to 0.125
Outputs:
- attn_grad: bfloat16 [16384, 2048], P(('dp', 'expert'))
- proj_grad: bfloat16 [2048, 2880], P('dp')
- down_grad: bfloat16 [32, 2880, 2880], P('expert', 'dp')
- logit_grad: float32 [16384, 4], P(('dp', 'expert'))
Inputs may be any that keep to these rules, and one draw needn't show every extreme that they name: `expert_ids`: each token names 4 different experts. Among the tokens of one device no expert is named more than 20 times, and in every draw some expert is named exactly 20 times by the tokens of some device.
All inputs are finite; a program needn't handle non-finite values.
Results may differ from a plain program's by a relative error of at most 0.019.
Values may be sent and summed in bfloat16 or wider, within the bound.
A program may use at most 192 MiB of HBM per device.

v0:
```python
import jax
import jax.numpy as jnp
from jax import lax
from jax.sharding import PartitionSpec as P


def slot_of(ids_flat, experts, cap):
    onehot = (ids_flat[:, None] == jnp.arange(experts, dtype=jnp.int32)[None, :]).astype(jnp.int32)
    before = jnp.cumsum(onehot, axis=0) - onehot
    return ids_flat * cap + jnp.sum(before * onehot, axis=1)


def owner_of(slots, count):
    owner = jnp.full((count,), -1, dtype=jnp.int32)
    return owner.at[slots].set(jnp.arange(slots.shape[0], dtype=jnp.int32))


def local(
    out_grad,
    expert_ids,
    chosen_logits,
    router_weight,
    hidden_act,
    down_weight,
    attn_out,
    proj_weight,
):
    n_data = lax.axis_size("dp")
    n_owner = lax.axis_size("expert")
    n_source = n_data * n_owner
    rows_dev, width = out_grad.shape
    top = expert_ids.shape[1]
    cap = hidden_act.shape[2]
    hidden = hidden_act.shape[3]
    expw = jnp.exp(chosen_logits)
    gates = expw / jnp.sum(expw, axis=1, keepdims=True)
    gate_b = gates.astype(jnp.bfloat16)
    slots = slot_of(expert_ids.reshape(-1), n_owner, cap)
    owners = owner_of(slots, n_owner * cap)
    valid = owners >= 0
    safe = jnp.maximum(owners, 0)
    send_rows = jnp.where(
        valid[:, None], out_grad[safe // top], jnp.zeros((), jnp.bfloat16)
    ).reshape(n_owner, cap, width)
    send_gate = jnp.where(valid, gate_b.reshape(-1)[safe], jnp.zeros((), jnp.bfloat16)).reshape(
        n_owner, cap
    )
    rows_all = jnp.broadcast_to(send_rows[None], (n_data, n_owner, cap, width)).reshape(
        n_source, cap, width
    )
    gate_all = jnp.broadcast_to(send_gate[None], (n_data, n_owner, cap)).reshape(n_source, cap)
    recv_rows, recv_gate = (
        lax.all_to_all(rows_all, ("dp", "expert"), split_axis=0, concat_axis=0, tiled=True),
        lax.all_to_all(gate_all, ("dp", "expert"), split_axis=0, concat_axis=0, tiled=True),
    )
    weight = down_weight[0]
    hid = hidden_act[0].reshape(n_source * cap, hidden)
    flat = recv_rows.reshape(n_source * cap, width)
    upward = lax.dot_general(
        flat, weight, (((1,), (1,)), ((), ())), preferred_element_type=jnp.float32
    )
    partial_grad = jnp.sum(upward * hid.astype(jnp.float32), axis=1).reshape(n_source, cap)
    scaled = (recv_gate[:, :, None] * recv_rows).reshape(n_source * cap, width)
    down_grad = lax.dot_general(
        hid, scaled, (((0,), (0,)), ((), ())), preferred_element_type=jnp.float32
    ).astype(jnp.bfloat16)[None]
    returned = lax.all_to_all(
        partial_grad, ("dp", "expert"), split_axis=0, concat_axis=0, tiled=True
    )
    slot_grad = jnp.sum(returned.reshape(n_data, n_owner, cap), axis=0)
    choice_grad = slot_grad.reshape(-1)[slots].reshape(rows_dev, top)
    logit_grad = gates * (choice_grad - jnp.sum(gates * choice_grad, axis=1, keepdims=True))
    table = (expert_ids[:, :, None] == jnp.arange(n_owner, dtype=jnp.int32)[None, None, :]).astype(
        jnp.float32
    )
    router_rows = jnp.sum(logit_grad[:, :, None] * table, axis=1).astype(jnp.bfloat16)
    back = lax.dot_general(
        router_rows, router_weight, (((1,), (1,)), ((), ())), preferred_element_type=jnp.float32
    )
    resid_grad = (out_grad.astype(jnp.float32) + back).astype(jnp.bfloat16)
    attn_grad = lax.dot_general(
        resid_grad,
        lax.all_gather(proj_weight, "dp", axis=0, tiled=True),
        (((1,), (1,)), ((), ())),
        preferred_element_type=jnp.float32,
    ).astype(jnp.bfloat16)
    sectioned = lax.psum_scatter(
        lax.dot_general(
            attn_out, resid_grad, (((0,), (0,)), ((), ())), preferred_element_type=jnp.float32
        ).astype(jnp.bfloat16),
        "dp",
        scatter_dimension=0,
        tiled=True,
    ).astype(jnp.float32)
    sectioned = lax.optimization_barrier(sectioned.astype(jnp.bfloat16)).astype(jnp.float32)
    total = lax.psum(sectioned.astype(jnp.bfloat16), "expert")
    return (attn_grad, total, down_grad, logit_grad)


def solution(mesh):
    return jax.shard_map(
        local,
        mesh=mesh,
        in_specs=(
            P(("dp", "expert"), None),
            P(("dp", "expert"), None),
            P(("dp", "expert"), None),
            P(),
            P("expert", None, None, "dp"),
            P("expert", "dp", None),
            P(("dp", "expert"), None),
            P("dp", None),
        ),
        out_specs=(
            P(("dp", "expert"), None),
            P("dp", None),
            P("expert", "dp", None),
            P(("dp", "expert"), None),
        ),
        check_vma=False,
    )
```

profile of v0, /device:TPU:1, one launch (start us, length us, event | category | flops | bytes accessed | tf_op | source)
XLA Modules:
  0.0 713.6 jit_solution(6289856825082133377)
XLA Ops:
  7.2 0.8 copy.58
  8.0 0.1 eq.45
  8.1 0.1 eq.41
  8.2 0.7 broadcast_multiply_fusion.1
  8.9 1.2 reduce-window.6
  10.1 0.2 slice_reduce_fusion
  10.4 0.1 copy.57
  10.5 0.1 mul.48
  10.7 2.4 scatter_custom_fusion
  13.2 0.7 exponential_reduce_fusion
  13.9 0.1 copy.56
  14.1 0.1 reshape.110
  14.2 4.3 gather_fusion.2
  18.6 0.1 broadcast_in_dim.53
  18.7 1.5 copy.61
  20.1 4.6 gather_fusion
  24.7 6.5 gather.12
  31.1 2.8 broadcast_select_fusion
  33.9 6.5 broadcast_in_dim.57
  40.4 11.9 %all-to-all-start = ((bf16[128,20,2880]{2,1,0:T(8,128)(2,1)}), bf16[128,20,2880]{2,1,0:T(8,128)(2,1)}, u32[]{:S(2)}, u32[]{:S(2)}) async-start(bf16[128,20,2880]{2,1,0:T(8,128)(2,1)} %bitcast.50), calls=%async_computation | async-start | bytes 36175872 | tf_op jit(solution)/shard_map/all_to_all | solution.py:53
  52.3 6.8 copy.62
  59.1 7.3 %reshape_squeeze.3 = bf16[2560,720]{1,0:T(8,128)(2,1)} reshape(bf16[1,128,20,720]{3,2,1,0:T(8,128)(2,1)} %copy.62) | data formatting | bytes 7372800 | tf_op jit(solution)/shard_map/reshape;squeeze | solution.py:57
  66.3 6.1 copy.63
  72.5 217.9 %all-to-all-done = bf16[128,20,2880]{2,1,0:T(8,128)(2,1)} async-done(((bf16[128,20,2880]{2,1,0:T(8,128)(2,1)}), bf16[128,20,2880]{2,1,0:T(8,128)(2,1)}, u32[]{:S(2)}, u32[]{:S(2)}) %all-to-all-start) | async-done | bytes 14745632 | tf_op jit(solution)/shard_map/all_to_all | solution.py:53
  290.4 21.1 %reshape.106 = bf16[2560,2880]{1,0:T(8,128)(2,1)} reshape(bf16[128,20,2880]{2,1,0:T(8,128)(2,1)} %all-to-all-done) | data formatting | bytes 29491200 | tf_op jit(solution)/shard_map/reshape | solution.py:58
  311.5 16.8 %multiply_reduce_fusion = f32[2560]{0:T(1024)S(1)} fusion(bf16[2560,720]{0,1:T(8,128)(2,1)} %copy.63, bf16[2560,2880]{1,0:T(8,128)(2,1)} %reshape.106, bf16[1,720,2880]{2,1,0:T(8,128)(2,1)} %param.13), kind=kOutput, calls=%fused_computation.6 | convolution fusion | flops 10622359552 | bytes 22589440 | tf_op jit(solution)/shard_map/dot_general | solution.py:59
  328.3 0.7 all_to_all.16
  329.0 23.2 %all-to-all-start.1 = ((f32[128,1,20]{2,1,0:T(1,128)}), f32[128,1,20]{2,1,0:T(1,128)S(1)}, u32[]{:S(2)}, u32[]{:S(2)}) async-start(f32[128,1,20]{2,1,0:T(1,128)} %bitcast.5), calls=%async_computation.1 | async-start | bytes 131072 | tf_op jit(solution)/shard_map/all_to_all | solution.py:67
  352.2 0.2 reduce-scatter.2.cloned.1.call-start
  352.4 9.1 %all-to-all-done.1 = f32[128,1,20]{2,1,0:T(1,128)S(1)} async-done(((f32[128,1,20]{2,1,0:T(1,128)}), f32[128,1,20]{2,1,0:T(1,128)S(1)}, u32[]{:S(2)}, u32[]{:S(2)}) %all-to-all-start.1) | async-done | bytes 10272 | tf_op jit(solution)/shard_map/all_to_all | solution.py:67
  361.6 2.3 gather_fusion.1
  363.9 0.1 reshape.109
  364.1 0.2 multiply_reduce_fusion.1
  364.2 0.1 subtract_multiply_fusion
  364.5 0.4 fusion.2
  364.9 6.0 convert_bitcast_fusion
  371.0 0.7 all-gather.2.cloned.1.call-update
  371.7 0.1 broadcast_in_dim.60
  372.0 0.1 copy.67
  372.2 13.8 %all_to_all.23 = bf16[128,1,20]{2,1,0:T(2,128)(2,1)S(1)} all-to-all(bf16[128,1,20]{2,1,0:T(2,128)(2,1)S(1)} %copy.67), channel_id=1, replica_groups=mesh['dp'=4,'expert'=32] {'dp','expert'}, dimensions={0} | all-to-all | bytes 10240 | tf_op jit(solution)/shard_map/all_to_all | solution.py:54
  386.0 16.7 %broadcast_multiply_fusion = bf16[128,20,2880]{2,1,0:T(8,128)(2,1)} fusion(bf16[128,20,2880]{2,1,0:T(8,128)(2,1)} %all-to-all-done, bf16[128,20]{1,0:T(8,128)(2,1)S(1)} %bitcast.52), kind=kLoop, calls=%fused_computation.5 | loop fusion | flops 7372800 | bytes 29496320 | tf_op jit(solution)/shard_map/mul | solution.py:63
  402.7 22.9 %reshape.111 = bf16[2560,2880]{1,0:T(8,128)(2,1)} reshape(bf16[128,20,2880]{2,1,0:T(8,128)(2,1)} %broadcast_multiply_fusion) | data formatting | bytes 29491200 | tf_op jit(solution)/shard_map/reshape | solution.py:63
  425.5 50.7 %reduce-scatter.2.cloned.1.call-done = bf16[512,2880]{0,1:T(8,128)(2,1)} async-done(((bf16[2048,2880]{0,1:T(8,128)(2,1)}), bf16[512,2880]{0,1:T(8,128)(2,1)}) %reduce-scatter.2.cloned.1.call-update) | async-done | bytes 2949136 | tf_op jit(solution)/shard_map/reduce_scatter | solution.py:87
  476.3 17.5 %fusion = bf16[1,720,2880]{2,1,0:T(8,128)(2,1)} fusion(bf16[2560,2880]{1,0:T(8,128)(2,1)} %reshape.111, bf16[2560,720]{1,0:T(8,128)(2,1)} %reshape_squeeze.3), kind=kOutput, calls=%fused_computation.9 | convolution fusion | flops 10618905600 | bytes 22579200 | tf_op jit(solution)/shard_map/dot_general | solution.py:64
  493.8 95.7 %all-gather.2.cloned.1.call-done = bf16[2048,2880]{0,1:T(8,128)(2,1)} async-done(((bf16[512,2880]{0,1:T(8,128)(2,1)}), bf16[2048,2880]{0,1:T(8,128)(2,1)}) %all-gather.2.cloned.1.call-update) | async-done | bytes 11796496 | tf_op jit(solution)/shard_map/all_gather | solution.py:83
  589.5 7.0 convolution_convert_fusion.1
  596.6 106.8 %all-reduce.2.cloned.1.call-done = bf16[512,2880]{0,1:T(8,128)(2,1)} async-done(((bf16[512,2880]{0,1:T(8,128)(2,1)}), bf16[512,2880]{0,1:T(8,128)(2,1)}) %all-reduce.2.cloned.1.call-update) | async-done | bytes 2949136 | tf_op jit(solution)/shard_map/psum | solution.py:96
  703.4 3.6 copy.78
  (35 shorter events, 0.8 us)
Async XLA Ops:
  7.2 357.7 %copy-start = (bf16[128,2048]{1,0:T(8,128)(2,1)S(1)}, bf16[128,2048]{1,0:T(8,128)(2,1)}, u32[]{:S(2)}) copy-start(bf16[128,2048]{1,0:T(8,128)(2,1)} %param.14) | copy-start | bytes 1572868
  40.4 250.0 %all-to-all-start = ((bf16[128,20,2880]{2,1,0:T(8,128)(2,1)}), bf16[128,20,2880]{2,1,0:T(8,128)(2,1)}, u32[]{:S(2)}, u32[]{:S(2)}) async-start(bf16[128,20,2880]{2,1,0:T(8,128)(2,1)} %bitcast.50), calls=%async_computation | async-start | bytes 36175872 | tf_op jit(solution)/shard_map/all_to_all | solution.py:53
  311.5 52.9 %copy-start.4 = (s32[128,4]{0,1:T(4,128)S(1)}, s32[128,4]{0,1:T(4,128)}, u32[]{:S(2)}) copy-start(s32[128,4]{0,1:T(4,128)} %param.9) | copy-start | bytes 6148
  311.5 53.0 %copy-start.2 = (bf16[128,2880]{0,1:T(8,128)(2,1)S(1)}, bf16[128,2880]{0,1:T(8,128)(2,1)}, u32[]{:S(2)}) copy-start(bf16[128,2880]{0,1:T(8,128)(2,1)} %param.8) | copy-start | bytes 2211844
  311.5 53.0 %copy-start.3 = (bf16[2880,32]{0,1:T(8,128)(2,1)S(1)}, bf16[2880,32]{0,1:T(8,128)(2,1)}, u32[]{:S(2)}) copy-start(bf16[2880,32]{0,1:T(8,128)(2,1)} %param.11) | copy-start | bytes 552964
  329.0 32.5 %all-to-all-start.1 = ((f32[128,1,20]{2,1,0:T(1,128)}), f32[128,1,20]{2,1,0:T(1,128)S(1)}, u32[]{:S(2)}, u32[]{:S(2)}) async-start(f32[128,1,20]{2,1,0:T(1,128)} %bitcast.5), calls=%async_computation.1 | async-start | bytes 131072 | tf_op jit(solution)/shard_map/all_to_all | solution.py:67
  352.2 124.1 %reduce-scatter.2.cloned.1.call-start = ((), (), s32[]{:S(2)}) async-start(), calls=%async_computation.5 | async-start | bytes 14745600 | tf_op jit(solution)/shard_map/reduce_scatter | solution.py:87
  364.4 6.5 copy-start.5
  370.9 218.6 %all-gather.2.cloned.1.call-start = ((), (), s32[]{:S(2)}) async-start(), calls=%async_computation.4 | async-start | bytes 14745600 | tf_op jit(solution)/shard_map/all_gather | solution.py:83
  371.7 331.7 %all-reduce.2.cloned.1.call-start = ((), (), s32[]{:S(2)}) async-start(), calls=%async_computation.6 | async-start | bytes 5898240 | tf_op jit(solution)/shard_map/psum | solution.py:96
  589.5 117.5 %copy-start.1 = (bf16[128,2048]{1,0:T(8,128)(2,1)S(1)}, bf16[128,2048]{1,0:T(8,128)(2,1)}, u32[]{:S(2)}) copy-start(bf16[128,2048]{1,0:T(8,128)(2,1)} %param.14) | copy-start | bytes 1572868
Sparse Core Ops, SparseCore 0:
  371.0 105.1 reduce-scatter.1
  477.9 111.5 all-gather.1
  592.9 110.4 all-reduce.1
where the time goes:
time: 716 us; the launch traced here: 714 us
  waiting for transfers between devices  481 us (67%)
  local copies, waits for them, and re-layouts  99 us (14%)
  matrix products  47.8 us (7%)
  starting transfers between devices  35.4 us (5%)
  other arithmetic  22.6 us (3%)
  between operations  14 us (2%)
  blocking collectives  13.8 us (2%)
    all_to_all x1, waiting for transfers between devices, local(): lax.all_to_all(rows_all, ('dp', 'expert'), split_axis=0, concat_axis=0, t...  218 us
    psum x1, waiting for transfers between devices, local(): total = lax.psum(sectioned.astype(jnp.bfloat16), 'expert')  107 us
    all_gather x1, waiting for transfers between devices, local(): lax.all_gather(proj_weight, 'dp', axis=0, tiled=True)  95.7 us
    reduce_scatter x1, waiting for transfers between devices, local(): lax.psum_scatter(lax.dot_general(attn_out, resid_grad, (((0,), (0,)), (()...  50.7 us
    all_to_all x1, starting transfers between devices, local(): lax.all_to_all(partial_grad, ('dp', 'expert'), split_axis=0, concat_axis=...  23.2 us
    reshape x1, local copies, waits for them, and re-layouts, local(): scaled = (recv_gate[:, :, None] * recv_rows).reshape(n_source * cap, width)  22.9 us
    reshape x1, local copies, waits for them, and re-layouts, local(): flat = recv_rows.reshape(n_source * cap, width)  21.1 us
    dot_general x1, matrix products, local(): lax.dot_general(hid, scaled, (((0,), (0,)), ((), ())), preferred_element_...  17.5 us
  transfers between devices with their start and end apart: 5, of which 5 were waited for; matrix products, arithmetic and copies ran while one was open for 12% of the time, Pallas kernels for 0%

commit v1 on v0

v1 whole, which is shorter than its diff:
```python
import functools

import jax
import jax.numpy as jnp
from jax import lax
from jax.experimental import pallas as pl
from jax.experimental.pallas import tpu as pltpu
from jax.sharding import PartitionSpec as P

MESH = pl.DeviceIdType.MESH
BF = jnp.bfloat16
F32 = jnp.float32
D = 2880
DP = 2944
MAIN = 2816
FF = 720
TOK = 128
NE = 32
CAP = 20
SEC = 512
HID = 2048
CH = 256
NA = 8
NC = 3
ROWS = 2560


def dot(a, b, ca, cb, precision=None):
    return lax.dot_general(
        a, b, (((ca,), (cb,)), ((), ())), preferred_element_type=F32, precision=precision
    )


def iota(shape, dim):
    return lax.broadcasted_iota(jnp.int32, shape, dim)


def place():
    y = lax.axis_index("dp")
    e = lax.axis_index("expert")
    x = lax.div(e, 8)
    z = lax.rem(lax.div(e, 2), 4)
    c = lax.rem(e, 2)
    return y, x, z, c


def dev(y, x, z, c):
    return (lax.rem(y, 4), lax.rem(x, 4) * 8 + lax.rem(z, 4) * 2 + c)


def remote(src, dst, ss, rs, to):
    return pltpu.make_async_remote_copy(
        src_ref=src, dst_ref=dst, send_sem=ss, recv_sem=rs, device_id=to, device_id_type=MESH
    )


def greet(peers):
    bar = pltpu.get_barrier_semaphore()
    for p in peers:
        pl.semaphore_signal(bar, inc=1, device_id=p, device_id_type=MESH)
    pl.semaphore_wait(bar, len(peers))


def dense_gates(ids_ref, log_ref):
    lane = iota((TOK, NE), 1)
    w = jnp.exp(log_ref[...])
    gates = w / jnp.sum(w, axis=1, keepdims=True)
    chosen = jnp.zeros((TOK, NE), F32)
    dense = jnp.zeros((TOK, NE), F32)
    for k in range(4):
        hit = ids_ref[:, k : k + 1] == lane
        chosen = chosen + jnp.where(hit, 1.0, 0.0)
        dense = dense + jnp.where(hit, gates[:, k : k + 1], 0.0)
    lower = jnp.where(iota((TOK, TOK), 1) < iota((TOK, TOK), 0), 1.0, 0.0).astype(BF)
    count = dot(lower, chosen.astype(BF), 1, 0)
    pos = jnp.where(chosen > 0.0, count, -1.0)
    return dense, pos


def shift_to(rows, start):
    return jnp.where(iota((rows, 128), 1) == iota((rows, 128), 0) + start, 1.0, 0.0).astype(BF)


def first_kernel(
    og, ids, logits, ao, pw, rw, yt, s1, mr, aos, rpt, ms, aot, rpo, ss, rs, ls
):
    y, x, z, c = place()
    peer = [dev(y + i, x, z, c) for i in (1, 2, 3)]
    dense, pos = dense_gates(ids, logits)
    side = (
        dot(og[:, MAIN:D], shift_to(64, 0), 1, 0)
        + dot(pos.astype(BF), shift_to(NE, 64), 1, 0)
        + dot(dense.astype(BF), shift_to(NE, 96), 1, 0)
    )
    yt[y, :, 0:MAIN] = og[:, 0:MAIN]
    yt[y, :, MAIN:DP] = side.astype(BF)
    greet(peer)

    def tok(i):
        return remote(yt.at[y], yt.at[y], ss.at[i], rs.at[i], peer[0 if i == 0 else 2])

    def fwd(i):
        src = lax.rem(y + (3 if i == 0 else 1), 4)
        part = yt.at[src, pl.ds(64 * i, 64)]
        return remote(part, part, ss.at[2 + i], rs.at[2 + i], peer[0 if i == 0 else 2])

    def sections(i):
        to = lax.rem(y + i + 1, 4)
        cols = pl.ds(pl.multiple_of(to * SEC, SEC), SEC)
        return remote(ao.at[:, cols], aos.at[y], ss.at[4 + i], rs.at[4 + i], peer[i])

    def rp(i):
        return remote(rpo, rpt.at[y], ss.at[7 + i], rs.at[7 + i], peer[i])

    def back(i):
        to = lax.rem(y + i + 1, 4)
        return remote(ms.at[to], mr.at[y], ss.at[10 + i], rs.at[10 + i], peer[i])

    tok(0).start()
    tok(1).start()
    for i in range(3):
        sections(i).start()
    own = pltpu.make_async_copy(
        ao.at[:, pl.ds(pl.multiple_of(y * SEC, SEC), SEC)], aos.at[y], ls.at[0]
    )
    own.start()
    rpo[...] = dot(pw[...], rw[...], 1, 0).astype(BF)
    for i in range(3):
        rp(i).start()
    rpt[y] = rpo[...]

    def proj(t):
        return dot(yt[t, :, 0:D], pw[...], 1, 1).astype(BF)

    mr[y] = proj(y)
    tok(0).wait_recv()
    fwd(0).start()
    tok(1).wait_recv()
    fwd(1).start()
    for i in (0, 2):
        to = lax.rem(y + i + 1, 4)
        ms[to] = proj(to)
        back(i).start()
    own.wait()
    for i in range(3):
        sections(i).wait_recv()
    eye = jnp.where(iota((SEC, SEC), 0) == iota((SEC, SEC), 1), 1.0, 0.0).astype(BF)
    for t in range(4):
        aot[:, t * TOK : (t + 1) * TOK] = dot(eye, aos[t], 1, 1).astype(BF)
    fwd(0).wait_recv()
    fwd(1).wait_recv()
    to = lax.rem(y + 2, 4)
    ms[to] = proj(to)
    back(1).start()

    @pl.loop(0, MAIN // CH)
    def _(k):
        cols = pl.ds(pl.multiple_of(k * CH, CH), CH)
        block = yt[:, :, cols].reshape(4 * TOK, CH)
        s1[:, cols] = dot(aot[...], block, 1, 0).astype(BF)

    last = yt[:, :, MAIN:DP].reshape(4 * TOK, 128)
    s1[:, MAIN:D] = dot(aot[...], last, 1, 0)[:, 0:64].astype(BF)
    for i in range(2):
        tok(i).wait_send()
        fwd(i).wait_send()
    for i in range(3):
        sections(i).wait_send()
        rp(i).wait()
        back(i).wait()


def second_kernel(
    yt, hid_h, w_h, ids, logits, mr, aos, rpt,
    dg, attn, lg, qt,
    za, zc, zs, sb, sa, sc, sss, ra, rc, rsd, w, hid, hgt, acc, stg, stl,
    vs, yr, xr, zr, cr, rr, q0, q1, q2, q3,
    a_s, a_r, c_s, c_r, t_s, t_r, ls,
):
    y, x, z, c = place()
    e = x * 8 + z * 2 + c
    zp = [dev(y, x, z + i, c) for i in (1, 2, 3)]
    xp = [dev(y, x + i, z, c) for i in (1, 2, 3)]
    yp = [dev(y + i, x, z, c) for i in (1, 2, 3)]
    cp = dev(y, x, z, 1 - c)
    in_w = pltpu.make_async_copy(w_h, w, ls.at[0])
    in_h = pltpu.make_async_copy(hid_h, hid, ls.at[1])
    in_w.start()
    in_h.start()
    greet(zp + xp + yp + [cp])

    def src_rows(zz, cc):
        return pl.ds(pl.multiple_of((zz * 2 + cc) * TOK, TOK), TOK)

    mine = src_rows(z, c)

    def cols_of(k):
        return pl.ds(pl.multiple_of(k * CH, CH), CH)

    def a_z(k, i):
        src = yt.at[y, :, cols_of(k)]
        to = cp if i == 3 else zp[i]
        return remote(src, za.at[k, mine], a_s.at[k, i], a_r.at[k, i], to)

    def a_own(k):
        return pltpu.make_async_copy(yt.at[y, :, cols_of(k)], za.at[k, mine], a_s.at[k, 14])

    def a_c(k, i):
        part = za.at[k, src_rows(lax.rem(z + 3 - i, 4), c)]
        return remote(part, part, a_s.at[k, 4 + i], a_r.at[k, 4 + i], cp)

    def x_rows(yy, xx):
        return pl.ds(pl.multiple_of(yy * 640 + xx * 160, 160), 160)

    def a_x(k, i):
        to = lax.rem(x + i + 1, 4)
        return remote(
            sa.at[k, to], ra.at[k, x_rows(y, x)], a_s.at[k, 7 + i], a_r.at[k, 7 + i], xp[i]
        )

    def a_xown(k):
        return pltpu.make_async_copy(sa.at[k, x], ra.at[k, x_rows(y, x)], a_s.at[k, 15])

    def a_y(k, i):
        part = ra.at[k, pl.ds(pl.multiple_of(y * 640, 640), 640)]
        return remote(part, part, a_s.at[k, 10 + i], a_r.at[k, 10 + i], yp[2 * i])

    def a_f(k, i):
        src = lax.rem(y + (3 if i == 0 else 1), 4)
        part = ra.at[k, pl.ds(pl.multiple_of(src * 640 + 320 * i, 320), 320)]
        return remote(part, part, a_s.at[k, 12 + i], a_r.at[k, 12 + i], yp[2 * i])

    def c_refs(j, tail):
        if tail:
            return yt.at[:, :, pl.ds(MAIN, 128)], zs, sss, rsd
        return yt.at[:, :, cols_of(NA + j)], zc.at[j], sc.at[j], rc.at[j]

    def c_z(j, i, tail=False):
        src, zb, _, _ = c_refs(j, tail)
        to = cp if i == 3 else zp[i]
        return remote(src, zb.at[:, mine], c_s.at[j, i], c_r.at[j, i], to)

    def c_own(j, tail=False):
        src, zb, _, _ = c_refs(j, tail)
        return pltpu.make_async_copy(src, zb.at[:, mine], c_s.at[j, 14])

    def c_c(j, i, tail=False):
        _, zb, _, _ = c_refs(j, tail)
        part = zb.at[:, src_rows(lax.rem(z + 3 - i, 4), c)]
        return remote(part, part, c_s.at[j, 4 + i], c_r.at[j, 4 + i], cp)

    def c_x(j, i, tail=False):
        _, _, sbuf, rbuf = c_refs(j, tail)
        to = lax.rem(x + i + 1, 4)
        return remote(
            sbuf.at[to], rbuf.at[:, x], c_s.at[j, 7 + i], c_r.at[j, 7 + i], xp[i]
        )

    def c_xown(j, tail=False):
        _, _, sbuf, rbuf = c_refs(j, tail)
        return pltpu.make_async_copy(sbuf.at[x], rbuf.at[:, x], c_s.at[j, 15])

    def picks(yy):
        row, lane = iota((8, 128), 0), iota((8, 128), 1)
        sel = jnp.where((lane == 64 + row * 8 + z * 2 + c) & (row < 4), 1.0, 0.0).astype(BF)
        pos = dot(sel, zs[yy], 1, 1)
        r, t = iota((160, 1024), 0), iota((160, 1024), 1)
        base = jnp.zeros((160, 1024), jnp.int32)
        for s in range(1, 8):
            base = base + jnp.where(r >= s * CAP, 1, 0)
        key = jnp.where(lax.shift_right_logical(t, 7) == base, r - base * CAP, -5).astype(F32)
        for xx in range(4):
            one = jnp.where(pos[xx : xx + 1, :] == key, 1.0, 0.0).astype(BF)
            sb[yy, xx * 160 : (xx + 1) * 160, :] = one

    def send_c(j, tail=False):
        _, zb, sbuf, _ = c_refs(j, tail)

        @pl.loop(0, 4)
        def _(yy):
            got = dot(sb[yy], zb[yy], 1, 0).astype(BF)
            for xx in range(4):
                sbuf[xx, yy] = got[xx * 160 : (xx + 1) * 160]

        for i in range(3):
            c_x(j, i, tail).start()
        c_xown(j, tail).start()

    def slot_part(rows, cols, width):
        @pl.loop(0, 4)
        def _(b):
            rb = pl.ds(pl.multiple_of(b * 640, 640), 640)
            g = dot(hid[rb, :], w[:, cols], 1, 0)
            prod = g * rows[rb].astype(F32)
            if width == CH:
                acc[rb, :] += prod[:, 0:128] + prod[:, 128:256]
            else:
                acc[rb, 0:width] += prod

    def put(slot, k):
        return pltpu.make_async_copy(stg.at[slot], dg.at[:, cols_of(k)], ls.at[2 + slot])

    def put_tail():
        return pltpu.make_async_copy(stl, dg.at[:, pl.ds(MAIN, 128)], ls.at[4])

    @pl.loop(-4, NA + 2)
    def _(t):
        @pl.when((t >= 0) & (t < NA))
        def _():
            a_xown(t).wait()
            for i in range(3):
                a_x(t, i).wait_recv()
            for i in range(2):
                a_y(t, i).start()

        @pl.when((t >= 1) & (t < NA + 1))
        def _():
            for i in range(2):
                a_y(t - 1, i).wait_recv()
                a_f(t - 1, i).start()

        @pl.when(t == -4)
        def _():
            for i in range(4):
                c_z(NC, i, True).start()
            c_own(NC, True).start()

        @pl.when(t == -3)
        def _():
            for i in range(3):
                c_z(NC, i, True).wait_recv()
                c_c(NC, i, True).start()

        @pl.when(t == -2)
        def _():
            c_own(NC, True).wait()
            c_z(NC, 3, True).wait_recv()
            for i in range(3):
                c_c(NC, i, True).wait_recv()
            picks(y)

        @pl.when((t >= -2) & (t < NA - 2))
        def _():
            k = t + 2
            a_own(k).wait()
            a_z(k, 3).wait_recv()
            for i in range(3):
                a_c(k, i).wait_recv()
            got = dot(sb[y], za[k], 1, 0).astype(BF)
            for xx in range(4):
                sa[k, xx] = got[xx * 160 : (xx + 1) * 160]
            for i in range(3):
                a_x(k, i).start()
            a_xown(k).start()

        @pl.when((t >= -3) & (t < NA - 3))
        def _():
            for i in range(3):
                a_z(t + 3, i).wait_recv()
                a_c(t + 3, i).start()

        @pl.when((t >= -4) & (t < NA - 4))
        def _():
            for i in range(4):
                a_z(t + 4, i).start()
            a_own(t + 4).start()

        @pl.when(t == -1)
        def _():
            for i in (1, 2, 3):
                picks(lax.rem(y + i, 4))
            send_c(NC, True)
            in_w.wait()
            in_h.wait()
            acc[...] = jnp.zeros_like(acc)
            eye = jnp.where(iota((FF, FF), 0) == iota((FF, FF), 1), 1.0, 0.0).astype(BF)

            @pl.loop(0, ROWS // 256)
            def _(b):
                rb = pl.ds(pl.multiple_of(b * 256, 256), 256)
                hgt[:, rb] = dot(eye, hid[rb, :], 1, 1).astype(BF)

        @pl.when(t == 1)
        def _():
            c_xown(NC, True).wait()
            for i in range(3):
                c_x(NC, i, True).wait_recv()
            rows = rsd[...].reshape(ROWS, 128)
            sel = jnp.where(iota((8, 128), 1) == 96 + e, 1.0, 0.0).astype(BF)
            gate = dot(sel, rows, 1, 1)[0:1, :]

            @pl.loop(0, FF // 16)
            def _(b):
                rb = pl.ds(pl.multiple_of(b * 16, 16), 16)
                hgt[rb, :] = (hgt[rb, :].astype(F32) * gate).astype(BF)

            stl[...] = dot(hgt[...], rows, 1, 0).astype(BF)
            put_tail().start()
            g = dot(hid[...], w[:, MAIN:D], 1, 0)
            acc[:, 0:64] += g * rows[:, 0:64].astype(F32)

        odd = lax.rem(t + 8, 2) == 1
        j0 = lax.div(t + 1, 2)
        j2 = lax.div(t - 1, 2)

        @pl.when(odd & (t >= -1) & (j0 < NC))
        def _():
            for i in range(4):
                c_z(j0, i).start()
            c_own(j0).start()

        @pl.when(jnp.logical_not(odd) & (t >= 0) & (lax.div(t, 2) < NC))
        def _():
            j1 = lax.div(t, 2)
            for i in range(3):
                c_z(j1, i).wait_recv()
                c_c(j1, i).start()

        @pl.when(odd & (t >= 1) & (j2 < NC))
        def _():
            c_own(j2).wait()
            c_z(j2, 3).wait_recv()
            for i in range(3):
                c_c(j2, i).wait_recv()
            send_c(j2)

        @pl.when(odd & (t >= 3) & (t < 3 + 2 * NC))
        def _():
            j = lax.div(t - 3, 2)
            c_xown(j).wait()
            for i in range(3):
                c_x(j, i).wait_recv()

            @pl.when(j > 0)
            def _():
                put(1, NA + j - 1).wait()

            stg[1] = dot(hgt[...], rc[j].reshape(ROWS, CH), 1, 0).astype(BF)
            put(1, NA + j).start()

            @pl.loop(0, 4)
            def _(b):
                rb = pl.ds(pl.multiple_of(b * 640, 640), 640)
                g = dot(hid[rb, :], w[:, cols_of(NA + j)], 1, 0)
                prod = g * rc[j, b].reshape(640, CH).astype(F32)
                acc[rb, :] += prod[:, 0:128] + prod[:, 128:256]

        @pl.when((t >= 2) & (t < NA + 2))
        def _():
            k = t - 2
            for i in range(2):
                a_f(k, i).wait_recv()

            @pl.when(k > 0)
            def _():
                put(0, k - 1).wait()

            stg[0] = dot(hgt[...], ra[k], 1, 0).astype(BF)
            put(0, k).start()

            @pl.loop(0, 4)
            def _(b):
                rb = pl.ds(pl.multiple_of(b * 640, 640), 640)
                g = dot(hid[rb, :], w[:, cols_of(k)], 1, 0)
                prod = g * ra[k, rb, :].astype(F32)
                acc[rb, :] += prod[:, 0:128] + prod[:, 128:256]

    exact = lax.Precision.HIGHEST
    r1 = iota((160, 128), 0)
    base = jnp.zeros((160, 128), jnp.int32)
    for s in range(1, 8):
        base = base + jnp.where(r1 >= s * CAP, 1, 0)
    at_slot = iota((160, 128), 1) == r1 - base * CAP
    r2 = iota((8, 160), 1)
    low = iota((8, 160), 0) * CAP
    fold = jnp.where((r2 >= low) & (r2 < low + CAP), 1.0, 0.0)
    for b in range(16):
        total = jnp.sum(acc[b * 160 : (b + 1) * 160, :], axis=1, keepdims=True)
        vs[b // 4, b % 4] = dot(fold, jnp.where(at_slot, total, 0.0), 1, 0, exact)

    def s_y(i):
        return remote(
            vs.at[lax.rem(y + i + 1, 4)], yr.at[i], t_s.at[i], t_r.at[i], yp[i]
        )

    def s_x(i):
        to = lax.rem(x + i + 1, 4)
        return remote(vs.at[0, to], xr.at[x], t_s.at[3 + i], t_r.at[3 + i], xp[i])

    def s_z(i):
        return remote(xr, zr.at[:, z], t_s.at[6 + i], t_r.at[6 + i], zp[i])

    def s_c():
        return remote(zr, cr.at[:, :, c], t_s.at[9], t_r.at[9], cp)

    def r_y(i):
        return remote(rr.at[y], rr.at[y], t_s.at[10 + i], t_r.at[10 + i], yp[i])

    def q_c():
        return remote(q0, q1, t_s.at[13], t_r.at[13], cp)

    def q_z(i):
        return remote(q2.at[0], q2.at[1 + i], t_s.at[14 + i], t_r.at[14 + i], zp[i])

    def q_x(i):
        return remote(q3.at[0], q3.at[1 + i], t_s.at[17 + i], t_r.at[17 + i], xp[i])

    for i in range(3):
        s_y(i).start()
    dense, pos = dense_gates(ids, logits)
    for i in range(3):
        s_y(i).wait()
    vs[0] = vs[y] + yr[0] + yr[1] + yr[2]
    for i in range(3):
        s_x(i).start()
    xr[x] = vs[0, x]
    for i in range(3):
        s_x(i).wait()
    for i in range(3):
        s_z(i).start()
    zr[:, z] = xr[...]
    for i in range(3):
        s_z(i).wait()
    s_c().start()
    cr[:, :, c] = zr[...]
    s_c().wait()
    got = cr[...].reshape(NE, 8, 128)
    got = jnp.sum(jnp.where(iota((NE, 8, 128), 1) == z * 2 + c, got, 0.0), axis=1)
    back = jnp.transpose(jnp.concatenate([got, jnp.zeros((96, 128), F32)], axis=0))
    grad = jnp.zeros((TOK, NE), F32)
    for s in range(CAP):
        grad = grad + jnp.where(pos == s, back[s : s + 1, 0:NE], 0.0)
    inner = jnp.sum(dense * grad, axis=1, keepdims=True)
    full = dense * (grad - inner)
    rrow = dot(full.astype(BF), shift_to(NE, 0), 1, 0).astype(BF)
    rr[y] = rrow
    for i in range(3):
        r_y(i).start()
    lane = iota((TOK, NE), 1)
    for k in range(4):
        hit = ids[:, k : k + 1] == lane
        lg[:, k : k + 1] = jnp.sum(jnp.where(hit, full, 0.0), axis=1, keepdims=True)
    for i in range(3):
        r_y(i).wait()
    q = jnp.zeros((NE, SEC), F32)
    for t in range(4):
        q = q + dot(rr[t], aos[t], 0, 0)[0:NE]
    q0[...] = q
    q_c().start()
    for t in range(4):
        more = dot(rrow[:, 0:NE], rpt[t], 1, 1)
        attn[:, t * SEC : (t + 1) * SEC] = (mr[t].astype(F32) + more).astype(BF)
    q_c().wait()
    q2[0] = q0[...] + q1[...]
    for i in range(3):
        q_z(i).start()
    for i in range(3):
        q_z(i).wait()
    q3[0] = (q2[0] + q2[1]) + (q2[2] + q2[3])
    for i in range(3):
        q_x(i).start()
    for i in range(3):
        q_x(i).wait()
    qt[...] = (q3[0] + q3[1]) + (q3[2] + q3[3])

    put(0, NA - 1).wait()
    put(1, NA + NC - 1).wait()
    put_tail().wait()

    @pl.loop(0, NA)
    def _(k):
        for i in range(4):
            a_z(k, i).wait_send()
        for i in range(3):
            a_c(k, i).wait_send()
            a_x(k, i).wait_send()
        for i in range(2):
            a_y(k, i).wait_send()
            a_f(k, i).wait_send()

    def drain(j, tail):
        for i in range(4):
            c_z(j, i, tail).wait_send()
        for i in range(3):
            c_c(j, i, tail).wait_send()
            c_x(j, i, tail).wait_send()

    @pl.loop(0, NC)
    def _(j):
        drain(j, False)

    drain(NC, True)


def local(
    out_grad, expert_ids, chosen_logits, router_weight, hidden_act, down_weight, attn_out, proj_weight
):
    vm = pl.BlockSpec(memory_space=pltpu.VMEM)
    hbm = pl.BlockSpec(memory_space=pl.ANY)
    sds = jax.ShapeDtypeStruct
    sem = pltpu.SemaphoreType.DMA
    yt, s1, mr, aos, rpt = pl.pallas_call(
        first_kernel,
        out_shape=(
            sds((4, TOK, DP), BF), sds((SEC, D), BF), sds((4, TOK, SEC), BF),
            sds((4, TOK, SEC), BF), sds((4, SEC, NE), BF),
        ),
        in_specs=[vm, vm, vm, hbm, vm, vm],
        out_specs=(vm,) * 5,
        scratch_shapes=[
            pltpu.VMEM((4, TOK, SEC), BF), pltpu.VMEM((SEC, SEC), BF), pltpu.VMEM((SEC, NE), BF),
            sem((13,)), sem((13,)), sem((1,)),
        ],
        compiler_params=pltpu.CompilerParams(
            collective_id=0, has_side_effects=True, vmem_limit_bytes=40 * 2**20
        ),
        cost_estimate=pl.CostEstimate(
            flops=7 * 10**9, bytes_accessed=16 * 10**6, transcendentals=0
        ),
        name="first",
    )(out_grad, expert_ids, chosen_logits, attn_out, proj_weight, router_weight)
    total = lax.psum(s1, "expert")
    hid = hidden_act[0].reshape(ROWS, FF)
    v = pltpu.VMEM
    dg, attn, lg, qt = pl.pallas_call(
        second_kernel,
        out_shape=(
            sds((FF, DP), BF), sds((TOK, HID), BF), sds((TOK, 4), F32), sds((NE, SEC), F32),
        ),
        in_specs=[hbm, hbm, hbm, vm, vm, vm, vm, vm],
        out_specs=(hbm, vm, vm, vm),
        scratch_shapes=[
            v((NA, 1024, CH), BF), v((NC, 4, 1024, CH), BF), v((4, 1024, 128), BF),
            v((4, 640, 1024), BF), v((NA, 4, 160, CH), BF), v((NC, 4, 4, 160, CH), BF),
            v((4, 4, 160, 128), BF), v((NA, ROWS, CH), BF), v((NC, 4, 4, 160, CH), BF),
            v((4, 4, 160, 128), BF), v((FF, D), BF), v((ROWS, FF), BF), v((FF, ROWS), BF),
            v((ROWS, 128), F32), v((2, FF, CH), BF), v((FF, 128), BF),
            v((4, 4, 8, 128), F32), v((3, 4, 8, 128), F32), v((4, 8, 128), F32),
            v((4, 4, 8, 128), F32), v((4, 4, 2, 8, 128), F32), v((4, TOK, 128), BF),
            v((NE, SEC), F32), v((NE, SEC), F32), v((4, NE, SEC), F32), v((4, NE, SEC), F32),
            sem((NA, 16)), sem((NA, 16)), sem((NC + 1, 16)), sem((NC + 1, 16)),
            sem((20,)), sem((20,)), sem((5,)),
        ],
        compiler_params=pltpu.CompilerParams(
            collective_id=1, has_side_effects=True, vmem_limit_bytes=62 * 2**20
        ),
        cost_estimate=pl.CostEstimate(
            flops=50 * 10**9, bytes_accessed=400 * 10**6, transcendentals=0
        ),
        name="second",
    )(yt, hid, down_weight[0], expert_ids, chosen_logits, mr, aos, rpt)
    more = dot(qt.astype(BF), router_weight, 0, 1)
    proj_grad = (total.astype(F32) + more).astype(BF)
    return attn, proj_grad, dg[:, :D][None], lg


def solution(mesh):
    return jax.shard_map(
        local,
        mesh=mesh,
        in_specs=(
            P(("dp", "expert"), None),
            P(("dp", "expert"), None),
            P(("dp", "expert"), None),
            P(),
            P("expert", None, None, "dp"),
            P("expert", "dp", None),
            P(("dp", "expert"), None),
            P("dp", None),
        ),
        out_specs=(
            P(("dp", "expert"), None),
            P("dp", None),
            P("expert", "dp", None),
            P(("dp", "expert"), None),
        ),
        check_vma=False,
    )
```

time: 716 us -> 281 us (0.39)
  waiting for transfers between devices: 481 us -> 0.02 us
  Pallas kernels: 0 us -> 223 us
  local copies, waits for them, and re-layouts: 99 us -> 40.2 us
  matrix products: 47.8 us -> 2.82 us
  starting transfers between devices: 35.4 us -> 0.04 us
  other arithmetic: 22.6 us -> 0 us
  blocking collectives: 13.8 us -> 0 us
    all_to_all x2 -> x0, waiting for transfers between devices: 227 us -> none  [the longest x1 218 us: local(): lax.all_to_all(rows_all, ('dp', 'expert'), split_axis=0, concat_axis=0, t...]
    pallas_call x0 -> x2, Pallas kernels: none -> 223 us  [the longest x1 176 us: local(): pl.pallas_call(second_kernel, out_shape=(sds((FF, DP), BF), sds((TOK, HID...]
    psum x1, waiting for transfers between devices: 107 us -> 0.01 us  [local(): total = lax.psum(s1, 'expert')]
    all_gather x1 -> x0, waiting for transfers between devices: 95.7 us -> none  [local(): lax.all_gather(proj_weight, 'dp', axis=0, tiled=True)]
    reduce_scatter x1 -> x0, waiting for transfers between devices: 50.7 us -> none  [local(): lax.psum_scatter(lax.dot_general(attn_out, resid_grad, (((0,), (0,)), (()...]
    dot_general x5 -> x1, matrix products: 47.8 us -> 2.82 us  [dot(): lax.dot_general(a, b, (((ca,), (cb,)), ((), ())), preferred_element_type=...]
    reshape x5 -> x0, local copies, waits for them, and re-layouts: 44.2 us -> none  [the longest x1 22.9 us: local(): scaled = (recv_gate[:, :, None] * recv_rows).reshape(n_source * cap, width)]
    all_to_all x2 -> x0, starting transfers between devices: 35.1 us -> none  [the longest x1 23.2 us: local(): lax.all_to_all(partial_grad, ('dp', 'expert'), split_axis=0, concat_axis=...]
  transfers between devices with their start and end apart: 5 -> 1, of which waited for: 5 -> 0; matrix products, arithmetic and copies ran while one was open for 12% -> 7% of each run, Pallas kernels for 0% -> 63%
where the time goes in v1:
time: 281 us; the launch traced here: 280 us
  Pallas kernels  223 us (79%)
  local copies, waits for them, and re-layouts  40.2 us (14%)
  between operations  14.1 us (5%)
  matrix products  2.82 us (1%)
    pallas_call x1, Pallas kernels, local(): pl.pallas_call(second_kernel, out_shape=(sds((FF, DP), BF), sds((TOK, HID...  176 us
    pallas_call x1, Pallas kernels, local(): pl.pallas_call(first_kernel, out_shape=(sds((4, TOK, DP), BF), sds((SEC,...  47.7 us
    unnamed x33, local copies, waits for them, and re-layouts  28.4 us
    another operation x1, local copies, waits for them, and re-layouts, local(): hid = hidden_act[0].reshape(ROWS, FF)  7.29 us
  transfers between devices with their start and end apart: 1, of which 0 were waited for; matrix products, arithmetic and copies ran while one was open for 7% of the time, Pallas kernels for 63%

profile of v1, /device:TPU:1, one launch (start us, length us, event | category | flops | bytes accessed | tf_op | source)
XLA Modules:
  0.0 280.5 jit_solution(15918968171300064093)
XLA Ops:
  7.2 0.0 all-reduce.2.cloned.1.call-start
  7.2 0.8 copy.24.ids
  8.0 0.0 copy-start.2
  8.0 0.8 copy.25.logits
  8.8 0.0 copy-start.3
  8.8 2.1 copy.27.rw
  10.9 2.3 copy.23.og
  13.2 3.3 %copy.26.pw = bf16[512,2880]{1,0:T(8,128)(2,1)S(1)} copy(bf16[512,2880]{0,1:T(8,128)(2,1)} %param.15) | data formatting | bytes 5898240 | tf_op args[7]
  16.5 0.0 copy-done.2
  16.5 0.0 copy-done.3
  16.5 0.0 copy-start
  16.5 1.1 copy-done
  17.7 0.0 copy-start.1
  17.7 1.1 copy-done.1
  18.8 0.0 copy-start.4
  18.8 1.0 copy-done.4
  19.8 47.7 %first.1 = (bf16[4,128,2944]{2,1,0:T(8,128)(2,1)S(1)}, bf16[512,2880]{1,0:T(8,128)(2,1)}, bf16[4,128,512]{2,1,0:T(8,128)(2,1)S(1)}, bf16[4,128,512]{2,1,0:T(8,128)(2,1)S(1)}, bf16[4,512,32]{2,1,0:T(8,128)(2,1)S(1)}) custom-call(bf16[128,2880]{1,0:T(8,128)(2,1)S(1)} %copy-done, s32[128,4]{1,0:T(8,128)S(1)} %copy.24.ids, f32[128,4]{1,0:T(8,128)S(1)} %copy.25.logits, ...), custom_call_target="tpu_custom_call" | custom-call | flops 7000000000 | bytes 16000000 | tf_op jit(solution)/shard_map/first/pallas_call | solution.py:602
  67.5 0.0 copy-start.5
  67.6 1.7 copy-done.5
  69.2 0.0 copy-start.6
  69.2 0.8 copy-done.6
  70.0 0.0 copy-start.7
  70.0 0.8 copy-done.7
  70.8 0.0 copy-start.8
  70.8 0.8 copy-done.8
  71.6 0.0 all-reduce.2.cloned.1.call-update
  71.6 6.7 %copy.28 = bf16[1,128,20,720]{3,2,1,0:T(8,128)(2,1)} copy(bf16[1,128,20,720]{1,3,2,0:T(8,128)(2,1)} %param.12) | data formatting | bytes 7372800 | tf_op args[4]
  78.3 7.3 %reshape_squeeze.3.hid_h = bf16[2560,720]{1,0:T(8,128)(2,1)} reshape(bf16[1,128,20,720]{3,2,1,0:T(8,128)(2,1)} %copy.28) | data formatting | bytes 7372800 | tf_op jit(solution)/shard_map/reshape;squeeze | solution.py:623
  85.6 175.6 %second.1 = (bf16[720,2944]{1,0:T(8,128)(2,1)}, bf16[128,2048]{1,0:T(8,128)(2,1)}, f32[128,4]{1,0:T(8,128)}, f32[32,512]{1,0:T(8,128)}) custom-call(bf16[4,128,2944]{2,1,0:T(8,128)(2,1)} %copy-done.5, bf16[2560,720]{1,0:T(8,128)(2,1)} %reshape_squeeze.3.hid_h, bf16[720,2880]{1,0:T(8,128)(2,1)} %bitcast.4, s32[128,4]{1,0:T(8,128)} %copy-done.2, ...), custom_call_target="tpu_custom_call" | custom-call | flops 49999998976 | bytes 400000000 | tf_op jit(solution)/shard_map/second/pallas_call | solution.py:625
  261.2 1.5 copy.33
  262.7 0.0 copy-start.9
  262.7 0.0 copy-start.11
  262.7 4.6 %slice_bitcast_fusion = bf16[1,720,2880]{2,1,0:T(8,128)(2,1)} fusion(bf16[720,2944]{1,0:T(8,128)(2,1)} %get-tuple-element.20), kind=kLoop, calls=%fused_computation.1 | loop fusion | bytes 8294400 | tf_op jit(solution)/shard_map/broadcast_in_dim | solution.py:654
  267.3 0.0 all-reduce.2.cloned.1.call-done
  267.3 0.0 copy-done.9
  267.3 0.0 copy-done.11
  267.3 2.8 %add_convert_fusion = bf16[512,2880]{1,0:T(8,128)(2,1)S(1)} fusion(bf16[512,2880]{1,0:T(8,128)(2,1)} %all-reduce.2.cloned.1.call-done, bf16[2880,32]{0,1:T(8,128)(2,1)S(1)} %copy-done.9, f32[32,512]{1,0:T(8,128)S(1)} %copy-done.11), kind=kOutput, calls=%fused_computation | convolution fusion | flops 98811904 | bytes 6148096 | tf_op jit(solution)/shard_map/dot_general | solution.py:29
  270.1 0.0 copy-start.10
  270.1 2.7 copy.32
  272.9 0.0 copy-done.10
  272.9 0.8 copy.37
Async XLA Ops:
  7.2 260.1 %all-reduce.2.cloned.1.call-start = ((), (), s32[]{:S(2)}) async-start(), calls=%async_computation | async-start | bytes 6029312 | tf_op jit(solution)/shard_map/psum | solution.py:622
  8.0 8.5 %copy-start.2 = (s32[128,4]{1,0:T(8,128)}, s32[128,4]{1,0:T(8,128)S(1)}, u32[]{:S(2)}) copy-start(s32[128,4]{1,0:T(8,128)S(1)} %copy.24.ids) | copy-start | bytes 6148
  8.8 7.7 %copy-start.3 = (f32[128,4]{1,0:T(8,128)}, f32[128,4]{1,0:T(8,128)S(1)}, u32[]{:S(2)}) copy-start(f32[128,4]{1,0:T(8,128)S(1)} %copy.25.logits) | copy-start | bytes 6148
  16.5 1.1 copy-start
  17.7 1.1 copy-start.1
  18.8 1.0 copy-start.4
  67.5 1.7 copy-start.5
  69.2 0.8 copy-start.6
  70.0 0.8 copy-start.7
  70.8 0.8 copy-start.8
  262.7 4.6 %copy-start.9 = (bf16[2880,32]{0,1:T(8,128)(2,1)S(1)}, bf16[2880,32]{0,1:T(8,128)(2,1)}, u32[]{:S(2)}) copy-start(bf16[2880,32]{0,1:T(8,128)(2,1)} %param.11) | copy-start | bytes 552964
  262.7 4.6 %copy-start.11 = (f32[32,512]{1,0:T(8,128)S(1)}, f32[32,512]{1,0:T(8,128)}, u32[]{:S(2)}) copy-start(f32[32,512]{1,0:T(8,128)} %get-tuple-element.19) | copy-start | bytes 196612
  270.1 2.7 copy-start.10
Sparse Core Ops, SparseCore 0:
  71.7 145.2 all-reduce.1

commit v2 on v0

v2 whole, which is shorter than its diff:
```python
import functools

import jax
import jax.numpy as jnp
from jax import lax
from jax.experimental import pallas as pl
from jax.experimental.pallas import tpu as pltpu
from jax.sharding import PartitionSpec as P

MESH = pl.DeviceIdType.MESH
BF = jnp.bfloat16
F32 = jnp.float32
D = 2880
DP = 2944
MAIN = 2816
FF = 720
TOK = 128
NE = 32
CAP = 20
SEC = 512
HID = 2048
CH = 256
NA = 7
NC = 4
CB = NA * CH
STEPS = 28
AT = {
    "gate_hidden": (18,),
    "tail_core": (10,),
    "a_core": (2, 3, 4, 7, 8, 13, 14),
    "a_work": (21, 22, 23, 24, 25, 26, 27),
    "send_sections": (4,),
    "attn_part": (17,),
    "known_part": (14,),
    "tail_pick": (11,),
    "a_send_z": (0, 1, 2, 4, 5, 7, 8),
    "tail_z": (5,),
    "tok_c_ring": (2,),
    "tok_a_send": (2,),
    "y_send": (7, 8, 9, 10, 11, 19, 20),
    "c_work": (20, 21, 24, 27),
    "c_core": (12, 15, 18, 24),
    "sum_core": (17,),
    "pack_hidden": (1,),
    "c_pick": (13, 17, 20, 25),
    "give_z": (25,),
    "give_core": (27,),
    "y_ring": (11, 15, 16, 17, 18, 24, 25),
    "sum_x": (24,),
    "c_send_z": (5, 12, 16, 18),
    "sum_z": (22,),
    "tok_a_ring": (8,),
    "pick_own": (2,),
    "tail_own_core": (1,),
    "a_pick": (2, 5, 6, 7, 8, 13, 14),
}
ROWS = 2560


def dot(a, b, ca, cb, precision=None):
    return lax.dot_general(
        a, b, (((ca,), (cb,)), ((), ())), preferred_element_type=F32, precision=precision
    )


def iota(shape, dim):
    return lax.broadcasted_iota(jnp.int32, shape, dim)


def place():
    y = lax.axis_index("dp")
    e = lax.axis_index("expert")
    x = lax.div(e, 8)
    z = lax.rem(lax.div(e, 2), 4)
    c = lax.rem(e, 2)
    return y, x, z, c


def dev(y, x, z, c):
    return (lax.rem(y, 4), lax.rem(x, 4) * 8 + lax.rem(z, 4) * 2 + c)


def remote(src, dst, ss, rs, to):
    return pltpu.make_async_remote_copy(
        src_ref=src, dst_ref=dst, send_sem=ss, recv_sem=rs, device_id=to, device_id_type=MESH
    )


def greet(peers):
    bar = pltpu.get_barrier_semaphore()
    for p in peers:
        pl.semaphore_signal(bar, inc=1, device_id=p, device_id_type=MESH)
    pl.semaphore_wait(bar, len(peers))


def dense_gates(ids, logits):
    row = iota((NE, TOK), 0)
    w = jnp.exp(logits[...])
    gates = w / jnp.sum(w, axis=0, keepdims=True)
    chosen = jnp.zeros((NE, TOK), F32)
    dense = jnp.zeros((NE, TOK), F32)
    for k in range(4):
        hit = ids[k : k + 1, :] == row
        chosen = chosen + jnp.where(hit, 1.0, 0.0)
        dense = dense + jnp.where(hit, gates[k : k + 1, :], 0.0)
    upper = jnp.where(iota((TOK, TOK), 0) < iota((TOK, TOK), 1), 1.0, 0.0).astype(BF)
    count = dot(chosen.astype(BF), upper, 1, 0)
    return dense, jnp.where(chosen > 0.0, count, -1.0)


def eye(n):
    return jnp.where(iota((n, n), 0) == iota((n, n), 1), 1.0, 0.0).astype(BF)


def kernel(
    og_h, ids_h, log_h, ao, pw_h, rw_h, hid_h, w_h,
    dg, total, ra, rc, attn, lg, qt,
    og, ids, logits, pw, rw, hp, yt, za, zc, zs, sb, sa, sc, sss, rsd, rbuf, w, hid, hgt, acc,
    stg, stl, aos, aot, ms, mr, rpo, rpt, s1, cb, zb_, p1, xb_, xg,
    vs, yr, xr, zr, cr, rr, q0, q1, q2, q3,
    a_s, a_r, c_s, c_r, k_s, k_r, g_s, g_r, t_s, t_r, ls,
):
    y, x, z, c = place()
    e = x * 8 + z * 2 + c
    zp = [dev(y, x, z + i, c) for i in (1, 2, 3)]
    xp = [dev(y, x + i, z, c) for i in (1, 2, 3)]
    yp = [dev(y + i, x, z, c) for i in (1, 2, 3)]
    cp = dev(y, x, z, 1 - c)
    loads = [
        pltpu.make_async_copy(a, b, ls.at[5 + n])
        for n, (a, b) in enumerate(
            [(og_h, og), (ids_h, ids), (log_h, logits), (rw_h, rw), (pw_h, pw), (w_h, w)]
        )
    ]

    def load_hid(b):
        return pltpu.make_async_copy(
            hid_h.at[pl.ds(b * 2, 2)], hp.at[lax.rem(b, 2)], ls.at[11 + lax.rem(b, 2)]
        )

    for l in loads:
        l.start()
    load_hid(0).start()
    load_hid(1).start()
    greet(zp + xp + yp + [cp])
    for l in loads[:3]:
        l.wait()
    dense, pos = dense_gates(ids, logits)
    side = [og[MAIN:D, :], pos.astype(BF), dense.astype(BF)]
    yt[0, :, MAIN:DP] = dot(eye(TOK), jnp.concatenate(side, axis=0), 1, 1).astype(BF)

    @pl.loop(0, MAIN // CH)
    def _(k):
        rows = pl.ds(pl.multiple_of(k * CH, CH), CH)
        yt[0, :, rows] = dot(eye(TOK), og[rows, :], 1, 1).astype(BF)

    def src_rows(zz, cc):
        return pl.ds(pl.multiple_of((zz * 2 + cc) * TOK, TOK), TOK)

    mine = src_rows(z, c)

    def cols_of(k):
        return pl.ds(pl.multiple_of(k * CH, CH), CH)

    def tok(part, i):
        cols = pl.ds(CB, DP - CB) if part == 0 else pl.ds(0, CB)
        n = part * 4 + i
        return remote(
            yt.at[0, :, cols], yt.at[3 if i == 0 else 1, :, cols], k_s.at[n], k_r.at[n], yp[2 * i]
        )

    def tok_f(part, i):
        cols = pl.ds(CB, DP - CB) if part == 0 else pl.ds(0, CB)
        n = part * 4 + 2 + i
        rows = pl.ds(64 * i, 64)
        return remote(
            yt.at[3 if i == 0 else 1, rows, cols], yt.at[2, rows, cols],
            k_s.at[n], k_r.at[n], yp[2 * i],
        )

    def sections(i):
        to = lax.rem(y + i + 1, 4)
        cols = pl.ds(pl.multiple_of(to * SEC, SEC), SEC)
        return remote(ao.at[:, cols], aos.at[3 - i], k_s.at[8 + i], k_r.at[8 + i], yp[i])

    def own_section():
        cols = pl.ds(pl.multiple_of(y * SEC, SEC), SEC)
        return pltpu.make_async_copy(ao.at[:, cols], aos.at[0], ls.at[13])

    def rp(i):
        return remote(rpo, rpt.at[y], k_s.at[11 + i], k_r.at[11 + i], yp[i])

    def back(i):
        return remote(ms.at[i], mr.at[y], k_s.at[14 + i], k_r.at[14 + i], yp[i])

    def a_z(k, i):
        to = cp if i == 3 else zp[i]
        return remote(
            yt.at[0, :, cols_of(k)], za.at[k, mine], a_s.at[k, i], a_r.at[k, i], to
        )

    def a_own(k):
        return pltpu.make_async_copy(yt.at[0, :, cols_of(k)], za.at[k, mine], a_s.at[k, 14])

    def a_c(k, i):
        part = za.at[k, src_rows(lax.rem(z + 3 - i, 4), c)]
        return remote(part, part, a_s.at[k, 4 + i], a_r.at[k, 4 + i], cp)

    def x_rows(yy, xx):
        return pl.ds(pl.multiple_of(yy * 640 + xx * 160, 160), 160)

    def a_x(k, i):
        to = lax.rem(x + i + 1, 4)
        return remote(
            sa.at[k, to], ra.at[k, x_rows(y, x)], a_s.at[k, 7 + i], a_r.at[k, 7 + i], xp[i]
        )

    def a_xown(k):
        return pltpu.make_async_copy(sa.at[k, x], ra.at[k, x_rows(y, x)], a_s.at[k, 15])

    def a_y(k, i):
        part = ra.at[k, pl.ds(pl.multiple_of(y * 640, 640), 640)]
        return remote(part, part, a_s.at[k, 10 + i], a_r.at[k, 10 + i], yp[2 * i])

    def a_f(k, i):
        src = lax.rem(y + (3 if i == 0 else 1), 4)
        part = ra.at[k, pl.ds(pl.multiple_of(src * 640 + 320 * i, 320), 320)]
        return remote(part, part, a_s.at[k, 12 + i], a_r.at[k, 12 + i], yp[2 * i])

    def c_z(j, i):
        to = cp if i == 3 else zp[i]
        return remote(
            yt.at[:, :, cols_of(NA + j)], zc.at[j, :, mine], c_s.at[j, i], c_r.at[j, i], to
        )

    def c_own(j):
        return pltpu.make_async_copy(
            yt.at[:, :, cols_of(NA + j)], zc.at[j, :, mine], c_s.at[j, 14]
        )

    def c_c(j, i):
        part = zc.at[j, :, src_rows(lax.rem(z + 3 - i, 4), c)]
        return remote(part, part, c_s.at[j, 4 + i], c_r.at[j, 4 + i], cp)

    def c_x(j, i):
        to = lax.rem(x + i + 1, 4)
        return remote(
            sc.at[lax.rem(j, 2), to], rc.at[j, :, x], c_s.at[j, 7 + i], c_r.at[j, 7 + i], xp[i]
        )

    def c_xown(j):
        return pltpu.make_async_copy(sc.at[lax.rem(j, 2), x], rc.at[j, :, x], c_s.at[j, 15])

    tail = pl.ds(MAIN, 128)

    def planes(part):
        return pl.ds(0, 1) if part == 0 else pl.ds(1, 3)

    def s_z(part, i):
        to = cp if i == 3 else zp[i]
        n = part * 7 + i
        return remote(
            yt.at[planes(part), :, tail], zs.at[planes(part), mine],
            c_s.at[NC, n], c_r.at[NC, n], to,
        )

    def s_own(part):
        return pltpu.make_async_copy(
            yt.at[planes(part), :, tail], zs.at[planes(part), mine], c_s.at[NC, 14 + part]
        )

    def s_c(part, i):
        n = part * 7 + 4 + i
        piece = zs.at[planes(part), src_rows(lax.rem(z + 3 - i, 4), c)]
        return remote(piece, piece, c_s.at[NC, n], c_r.at[NC, n], cp)

    def s_x(i):
        to = lax.rem(x + i + 1, 4)
        return remote(sss.at[to], rsd.at[:, x], c_s.at[NC + 1, i], c_r.at[NC + 1, i], xp[i])

    def s_xown():
        return pltpu.make_async_copy(sss.at[x], rsd.at[:, x], c_s.at[NC + 1, 14])

    def picks(i):
        row, lane = iota((8, 128), 0), iota((8, 128), 1)
        sel = jnp.where((lane == 64 + row * 8 + z * 2 + c) & (row < 4), 1.0, 0.0).astype(BF)
        slot = dot(sel, zs[i], 1, 1)
        r, t = iota((160, 1024), 0), iota((160, 1024), 1)
        key = jnp.where(
            lax.shift_right_logical(t, 7) == (r & 7), lax.shift_right_logical(r, 3), -5
        ).astype(F32)
        for xx in range(4):
            one = jnp.where(slot[xx : xx + 1, :] == key, 1.0, 0.0).astype(BF)
            sb[i, xx * 160 : (xx + 1) * 160, :] = one

    def g_core():
        there = pl.ds(pl.multiple_of((1 - c) * 256, 256), 256)
        return remote(s1.at[there], cb, g_s.at[0], g_r.at[0], cp)

    def g_z(i):
        to = lax.rem(z + i + 1, 4)
        rows = pl.ds(pl.multiple_of(c * 256 + to * 64, 64), 64)
        return remote(s1.at[rows], zb_.at[i], g_s.at[1 + i], g_r.at[1 + i], zp[i])

    def g_x(i):
        to = lax.rem(x + i + 1, 4)
        rows = pl.ds(pl.multiple_of(to * 16, 16), 16)
        return remote(p1.at[rows], xb_.at[i], g_s.at[4 + i], g_r.at[4 + i], xp[i])

    def h_x(i):
        rows = pl.ds(pl.multiple_of(x * 16, 16), 16)
        return remote(xg.at[rows], xg.at[rows], g_s.at[7 + i], g_r.at[7 + i], xp[i])

    at_z = pl.ds(pl.multiple_of(c * 256 + z * 64, 64), 64)

    def h_z(i):
        return remote(xg, total.at[at_z], g_s.at[10 + i], g_r.at[10 + i], zp[i])

    def h_own():
        return pltpu.make_async_copy(xg, total.at[at_z], g_s.at[14])

    def h_core():
        half = total.at[pl.ds(pl.multiple_of(c * 256, 256), 256)]
        return remote(half, half, g_s.at[13], g_r.at[13], cp)

    def hidden(b):
        return hid[pl.ds(b * 4, 4)].reshape(640, FF)

    def put(slot, k):
        return pltpu.make_async_copy(stg.at[slot], dg.at[:, cols_of(k)], ls.at[slot])

    def put_tail():
        return pltpu.make_async_copy(stl, dg.at[:, pl.ds(MAIN, 64)], ls.at[2])

    def work(slot, k):
        stg[slot] = dot(hgt[...], rbuf[slot], 1, 0).astype(BF)
        put(slot, k).start()

        @pl.loop(0, 4)
        def _(b):
            rb = pl.ds(pl.multiple_of(b * 640, 640), 640)
            g = dot(hidden(b), w[:, cols_of(k)], 1, 0)
            prod = g * rbuf[slot, rb, :].astype(F32)
            acc[rb, :] += prod[:, 0:128] + prod[:, 128:256]

    for i in range(4):
        s_z(0, i).start()
    s_own(0).start()
    for i in range(2):
        tok(0, i).start()

    def gate_hidden(_):
        s_xown().wait()
        for i in range(3):
            s_x(i).wait_recv()
        rows = rsd[...].reshape(ROWS, 128)
        sel = jnp.where(iota((8, 128), 1) == 96 + e, 1.0, 0.0).astype(BF)
        gate = dot(sel, rows, 1, 1)[0:1, :]

        @pl.loop(0, FF // 16)
        def _(b):
            rb = pl.ds(pl.multiple_of(b * 16, 16), 16)
            hgt[rb, :] = (hgt[rb, :].astype(F32) * gate).astype(BF)

        stl[...] = dot(hgt[...], rows, 1, 0)[:, 0:64].astype(BF)
        put_tail().start()
        @pl.loop(0, 4)
        def _(b):
            rb = pl.ds(pl.multiple_of(b * 640, 640), 640)
            g = dot(hidden(b), w[:, MAIN:D], 1, 0)
            part = rsd[b].reshape(640, 128)[:, 0:64].astype(F32)
            acc[rb, :] = jnp.concatenate([g * part, jnp.zeros((640, 64), F32)], axis=1)

    def tail_core(_):
        for i in range(3):
            s_z(1, i).wait_recv()
            s_c(1, i).start()

    def a_core(k):
        for i in range(3):
            a_z(k, i).wait_recv()
            a_c(k, i).start()

    def a_work(k):
        for i in range(2):
            a_f(k, i).wait_recv()
        fetch = pltpu.make_async_copy(ra.at[k], rbuf.at[0], ls.at[3])
        fetch.start()

        @pl.when(k > 0)
        def _():
            put(0, k - 1).wait()

        fetch.wait()
        work(0, k)

    def send_sections(_):
        for i in range(3):
            sections(i).start()
        own_section().start()

    def attn_part(_):
        @pl.loop(0, 4)
        def _(i):
            got = dot(yt[i, :, 0:D], pw[...], 1, 0).astype(BF)
            ms[lax.rem(i + 3, 4)] = got

        for i in range(3):
            back(i).start()
        mr[y] = ms[3]

    def known_part(_):
        for i in range(2):
            tok_f(1, i).wait_recv()
        own_section().wait()
        for i in range(3):
            sections(i).wait_recv()
        unit = eye(SEC)
        for i in range(4):
            aot[:, i * TOK : (i + 1) * TOK] = dot(unit, aos[i], 1, 1).astype(BF)

        @pl.loop(0, MAIN // CH)
        def _(k):
            block = yt[:, :, cols_of(k)].reshape(4 * TOK, CH)
            s1[:, cols_of(k)] = dot(aot[...], block, 1, 0).astype(BF)

        last = yt[:, :, MAIN:DP].reshape(4 * TOK, 128)
        s1[:, MAIN:D] = dot(aot[...], last, 1, 0)[:, 0:64].astype(BF)
        g_core().start()

    def tail_pick(_):
        s_own(1).wait()
        s_z(1, 3).wait_recv()
        for i in range(3):
            s_c(1, i).wait_recv()

        @pl.loop(1, 4)
        def _(i):
            picks(i)

        @pl.loop(0, 4)
        def _(i):
            got = dot(sb[i], zs[i], 1, 0).astype(BF)
            for xx in range(4):
                sss[xx, lax.rem(y + i, 4)] = got[xx * 160 : (xx + 1) * 160]

        for i in range(3):
            s_x(i).start()
        s_xown().start()

    def a_send_z(k):
        for i in range(4):
            a_z(k, i).start()
        a_own(k).start()

    def tail_z(_):
        for i in range(2):
            tok_f(0, i).wait_recv()
        for i in range(4):
            s_z(1, i).start()
        s_own(1).start()

    def tok_c_ring(_):
        for i in range(2):
            tok(0, i).wait_recv()
            tok_f(0, i).start()

    def tok_a_send(_):
        for i in range(2):
            tok(1, i).start()

    def y_send(k):
        a_xown(k).wait()
        for i in range(3):
            a_x(k, i).wait_recv()
        for i in range(2):
            a_y(k, i).start()

    def c_work(j):
        c_xown(j).wait()
        for i in range(3):
            c_x(j, i).wait_recv()
        fetches = [
            pltpu.make_async_copy(
                rc.at[j, yy, xx], rbuf.at[1, pl.ds(yy * 640 + xx * 160, 160)],
                ls.at[16 + yy * 4 + xx],
            )
            for yy in range(4) for xx in range(4)
        ]
        for f in fetches:
            f.start()

        @pl.when(j > 0)
        def _():
            put(1, NA + j - 1).wait()

        for f in fetches:
            f.wait()
        work(1, NA + j)

    def c_core(j):
        for i in range(3):
            c_z(j, i).wait_recv()
            c_c(j, i).start()

    def sum_core(_):
        g_core().wait()

        @pl.loop(0, 4)
        def _(b):
            here = pl.ds(pl.multiple_of(c * 256 + b * 64, 64), 64)
            there = pl.ds(pl.multiple_of(b * 64, 64), 64)
            s1[here, :] = (s1[here, :].astype(F32) + cb[there, :].astype(F32)).astype(BF)

        for i in range(3):
            g_z(i).start()

    def pack_hidden(_):
        @pl.loop(0, CAP // 2)
        def _(b):
            load_hid(b).wait()
            two = [
                dot(eye(TOK), hp[lax.rem(b, 2), h], 1, 1).reshape(16, 8, FF) for h in range(2)
            ]
            rows = pl.ds(pl.multiple_of(b * 16, 16), 16)
            hid[:, rows, :] = jnp.concatenate(two, axis=1).astype(BF)

            @pl.when(b < CAP // 2 - 2)
            def _():
                load_hid(b + 2).start()

        unit = eye(FF)

        @pl.loop(0, 4)
        def _(b):
            rb = pl.ds(pl.multiple_of(b * 640, 640), 640)
            hgt[:, rb] = dot(unit, hidden(b), 1, 1).astype(BF)

        loads[3].wait()
        loads[4].wait()
        loads[5].wait()
        rpo[...] = dot(rw[...], pw[...], 1, 0).astype(BF)
        for i in range(3):
            rp(i).start()
        rpt[y] = rpo[...]

    def c_pick(j):
        c_own(j).wait()
        c_z(j, 3).wait_recv()
        for i in range(3):
            c_c(j, i).wait_recv()

        @pl.when(j >= 2)
        def _():
            for i in range(3):
                c_x(j - 2, i).wait_send()

        @pl.loop(0, 4)
        def _(i):
            got = dot(sb[i], zc[j, i], 1, 0).astype(BF)
            for xx in range(4):
                sc[lax.rem(j, 2), xx, lax.rem(y + i, 4)] = got[xx * 160 : (xx + 1) * 160]

        for i in range(3):
            c_x(j, i).start()
        c_xown(j).start()

    def give_z(_):
        for i in range(3):
            h_x(i).wait_recv()
        for i in range(3):
            h_z(i).start()
        h_own().start()

    def give_core(_):
        for i in range(3):
            h_z(i).wait_recv()
        h_own().wait()
        h_core().start()

    def y_ring(k):
        for i in range(2):
            a_y(k, i).wait_recv()
            a_f(k, i).start()

    def sum_x(_):
        for i in range(3):
            g_x(i).wait_recv()
        rows = pl.ds(pl.multiple_of(x * 16, 16), 16)
        add = p1[rows, :].astype(F32) + xb_[0].astype(F32)
        xg[rows, :] = (add + (xb_[1].astype(F32) + xb_[2].astype(F32))).astype(BF)
        for i in range(3):
            h_x(i).start()

    def c_send_z(j):
        for i in range(4):
            c_z(j, i).start()
        c_own(j).start()

    def sum_z(_):
        for i in range(3):
            g_z(i).wait_recv()
        add = s1[at_z, :].astype(F32) + zb_[0].astype(F32)
        p1[...] = (add + (zb_[1].astype(F32) + zb_[2].astype(F32))).astype(BF)
        for i in range(3):
            g_x(i).start()

    def tok_a_ring(_):
        for i in range(2):
            tok(1, i).wait_recv()
            tok_f(1, i).start()

    def pick_own(_):
        s_own(0).wait()
        s_z(0, 3).wait_recv()
        for i in range(3):
            s_c(0, i).wait_recv()
        picks(0)

    def tail_own_core(_):
        for i in range(3):
            s_z(0, i).wait_recv()
            s_c(0, i).start()

    def a_pick(k):
        a_own(k).wait()
        a_z(k, 3).wait_recv()
        for i in range(3):
            a_c(k, i).wait_recv()
        got = dot(sb[0], za[k], 1, 0).astype(BF)
        for xx in range(4):
            sa[k, xx] = got[xx * 160 : (xx + 1) * 160]
        for i in range(3):
            a_x(k, i).start()
        a_xown(k).start()

    parts = {
        "gate_hidden": gate_hidden,
        "tail_core": tail_core,
        "a_core": a_core,
        "a_work": a_work,
        "send_sections": send_sections,
        "attn_part": attn_part,
        "known_part": known_part,
        "tail_pick": tail_pick,
        "a_send_z": a_send_z,
        "tail_z": tail_z,
        "tok_c_ring": tok_c_ring,
        "tok_a_send": tok_a_send,
        "y_send": y_send,
        "c_work": c_work,
        "c_core": c_core,
        "sum_core": sum_core,
        "pack_hidden": pack_hidden,
        "c_pick": c_pick,
        "give_z": give_z,
        "give_core": give_core,
        "y_ring": y_ring,
        "sum_x": sum_x,
        "c_send_z": c_send_z,
        "sum_z": sum_z,
        "tok_a_ring": tok_a_ring,
        "pick_own": pick_own,
        "tail_own_core": tail_own_core,
        "a_pick": a_pick,
    }

    @pl.loop(0, STEPS)
    def _(t):
        for key, at in AT.items():
            due = t == at[0]
            number = jnp.int32(0)
            for step in at[1:]:
                due = due | (t == step)
                number = number + jnp.where(t >= step, 1, 0)

            @pl.when(due)
            def _(part=parts[key], number=number):
                part(number)

    exact = lax.Precision.HIGHEST
    at_slot = iota((160, 128), 1) == lax.shift_right_logical(iota((160, 128), 0), 3)
    fold = jnp.where((iota((8, 160), 1) & 7) == iota((8, 160), 0), 1.0, 0.0)
    for b in range(16):
        sums = jnp.sum(acc[b * 160 : (b + 1) * 160, :], axis=1, keepdims=True)
        vs[b // 4, b % 4] = dot(fold, jnp.where(at_slot, sums, 0.0), 1, 0, exact)

    def v_y(i):
        return remote(
            vs.at[lax.rem(y + i + 1, 4)], yr.at[i], t_s.at[i], t_r.at[i], yp[i]
        )

    def v_x(i):
        to = lax.rem(x + i + 1, 4)
        return remote(vs.at[0, to], xr.at[x], t_s.at[3 + i], t_r.at[3 + i], xp[i])

    def v_z(i):
        return remote(xr, zr.at[:, z], t_s.at[6 + i], t_r.at[6 + i], zp[i])

    def v_c():
        return remote(zr, cr.at[:, :, c], t_s.at[9], t_r.at[9], cp)

    def r_y(i):
        return remote(rr.at[0], rr.at[3 - i], t_s.at[10 + i], t_r.at[10 + i], yp[i])

    def q_c():
        return remote(q0, q1, t_s.at[13], t_r.at[13], cp)

    def q_z(i):
        return remote(q2.at[0], q2.at[1 + i], t_s.at[14 + i], t_r.at[14 + i], zp[i])

    def q_x(i):
        return remote(q3.at[0], q3.at[1 + i], t_s.at[17 + i], t_r.at[17 + i], xp[i])

    for i in range(3):
        v_y(i).start()
    for i in range(3):
        v_y(i).wait()
    vs[0] = vs[y] + yr[0] + yr[1] + yr[2]
    for i in range(3):
        v_x(i).start()
    xr[x] = vs[0, x]
    for i in range(3):
        v_x(i).wait()
    for i in range(3):
        v_z(i).start()
    zr[:, z] = xr[...]
    for i in range(3):
        v_z(i).wait()
    v_c().start()
    cr[:, :, c] = zr[...]
    v_c().wait()
    got = cr[...].reshape(NE, 8, 128)
    got = jnp.sum(jnp.where(iota((NE, 8, 128), 1) == z * 2 + c, got, 0.0), axis=1)
    grad = jnp.zeros((NE, TOK), F32)
    for s in range(CAP):
        grad = grad + jnp.where(pos == s, got[:, s : s + 1], 0.0)
    inner = jnp.sum(dense * grad, axis=0, keepdims=True)
    full = dense * (grad - inner)
    rrow = full.astype(BF)
    rr[0] = rrow
    for i in range(3):
        r_y(i).start()
    row = iota((NE, TOK), 0)
    for k in range(4):
        hit = ids[k : k + 1, :] == row
        lg[k : k + 1, :] = jnp.sum(jnp.where(hit, full, 0.0), axis=0, keepdims=True)
    for i in range(3):
        r_y(i).wait()
    q = jnp.zeros((NE, SEC), F32)
    for t in range(4):
        q = q + dot(rr[t], aos[t], 1, 0)
    q0[...] = q
    q_c().start()
    for i in range(3):
        rp(i).wait()
        back(i).wait()
    for t in range(4):
        more = dot(rrow, rpt[t], 0, 0)
        attn[:, t * SEC : (t + 1) * SEC] = (mr[t].astype(F32) + more).astype(BF)
    q_c().wait()
    q2[0] = q0[...] + q1[...]
    for i in range(3):
        q_z(i).start()
    for i in range(3):
        q_z(i).wait()
    q3[0] = (q2[0] + q2[1]) + (q2[2] + q2[3])
    for i in range(3):
        q_x(i).start()
    for i in range(3):
        q_x(i).wait()
    qt[...] = (q3[0] + q3[1]) + (q3[2] + q3[3])

    put(0, NA - 1).wait()
    put(1, NA + NC - 1).wait()
    put_tail().wait()
    h_core().wait()
    for i in range(2):
        for part in range(2):
            tok(part, i).wait_send()
            tok_f(part, i).wait_send()
    for i in range(3):
        sections(i).wait_send()
        g_z(i).wait_send()
        g_x(i).wait_send()
        h_x(i).wait_send()
        h_z(i).wait_send()
        s_x(i).wait_send()
    for part in range(2):
        for i in range(4):
            s_z(part, i).wait_send()
        for i in range(3):
            s_c(part, i).wait_send()

    @pl.loop(0, NA)
    def _(k):
        for i in range(4):
            a_z(k, i).wait_send()
        for i in range(3):
            a_c(k, i).wait_send()
            a_x(k, i).wait_send()
        for i in range(2):
            a_y(k, i).wait_send()
            a_f(k, i).wait_send()

    @pl.loop(0, NC)
    def _(j):
        for i in range(4):
            c_z(j, i).wait_send()
        for i in range(3):
            c_c(j, i).wait_send()

        @pl.when(j >= NC - 2)
        def _():
            for i in range(3):
                c_x(j, i).wait_send()


def local(
    out_grad, expert_ids, chosen_logits, router_weight, hidden_act, down_weight, attn_out, proj_weight
):
    vm = pl.BlockSpec(memory_space=pltpu.VMEM)
    hbm = pl.BlockSpec(memory_space=pl.ANY)
    sds = jax.ShapeDtypeStruct
    sem = pltpu.SemaphoreType.DMA
    v = pltpu.VMEM
    dg, total, _, _, attn, lg, qt = pl.pallas_call(
        kernel,
        out_shape=(
            sds((FF, D), BF), sds((SEC, D), BF), sds((NA, ROWS, CH), BF),
            sds((NC, 4, 4, 160, CH), BF), sds((TOK, HID), BF), sds((4, TOK), F32),
            sds((NE, SEC), F32),
        ),
        in_specs=[hbm] * 8,
        out_specs=(hbm, hbm, hbm, hbm, vm, vm, vm),
        scratch_shapes=[
            v((D, TOK), BF), v((4, TOK), jnp.int32), v((4, TOK), F32), v((D, SEC), BF),
            v((NE, D), BF), v((2, 2, FF, TOK), BF), v((4, TOK, DP), BF),
            v((NA, 1024, CH), BF), v((NC, 4, 1024, CH), BF), v((4, 1024, 128), BF),
            v((4, 640, 1024), BF), v((NA, 4, 160, CH), BF), v((2, 4, 4, 160, CH), BF),
            v((4, 4, 160, 128), BF), v((4, 4, 160, 128), BF), v((2, ROWS, CH), BF),
            v((FF, D), BF), v((16, 160, FF), BF), v((FF, ROWS), BF),
            v((ROWS, 128), F32), v((2, FF, CH), BF), v((FF, 64), BF),
            v((4, TOK, SEC), BF), v((SEC, SEC), BF), v((4, TOK, SEC), BF), v((4, TOK, SEC), BF),
            v((NE, SEC), BF), v((4, NE, SEC), BF), v((SEC, D), BF), v((256, D), BF),
            v((3, 64, D), BF), v((64, D), BF), v((3, 16, D), BF), v((64, D), BF),
            v((4, 4, 8, 128), F32), v((3, 4, 8, 128), F32), v((4, 8, 128), F32),
            v((4, 4, 8, 128), F32), v((4, 4, 2, 8, 128), F32), v((4, NE, TOK), BF),
            v((NE, SEC), F32), v((NE, SEC), F32), v((4, NE, SEC), F32), v((4, NE, SEC), F32),
            sem((NA, 16)), sem((NA, 16)), sem((NC + 2, 16)), sem((NC + 2, 16)),
            sem((17,)), sem((17,)), sem((15,)), sem((15,)), sem((20,)), sem((20,)), sem((32,)),
        ],
        compiler_params=pltpu.CompilerParams(
            collective_id=0, has_side_effects=True, vmem_limit_bytes=62 * 2**20
        ),
        cost_estimate=pl.CostEstimate(
            flops=50 * 10**9, bytes_accessed=400 * 10**6, transcendentals=0
        ),
        name="layer_backward",
    )(
        out_grad.T, expert_ids.T, chosen_logits.T, attn_out, proj_weight.T, router_weight.T,
        jnp.transpose(hidden_act[0], (1, 2, 0)), down_weight[0],
    )
    more = dot(qt.astype(BF), router_weight, 0, 1)
    proj_grad = (total.astype(F32) + more).astype(BF)
    return attn, proj_grad, dg[None], lg.T


def solution(mesh):
    return jax.shard_map(
        local,
        mesh=mesh,
        in_specs=(
            P(("dp", "expert"), None),
            P(("dp", "expert"), None),
            P(("dp", "expert"), None),
            P(),
            P("expert", None, None, "dp"),
            P("expert", "dp", None),
            P(("dp", "expert"), None),
            P("dp", None),
        ),
        out_specs=(
            P(("dp", "expert"), None),
            P("dp", None),
            P("expert", "dp", None),
            P(("dp", "expert"), None),
        ),
        check_vma=False,
    )
```

time: 716 us -> 195 us (0.27)
  waiting for transfers between devices: 481 us -> 0 us
  Pallas kernels: 0 us -> 182 us
  local copies, waits for them, and re-layouts: 99 us -> 8.64 us
  matrix products: 47.8 us -> 2.87 us
  starting transfers between devices: 35.4 us -> 0 us
  other arithmetic: 22.6 us -> 0 us
  blocking collectives: 13.8 us -> 0 us
  between operations: 14 us -> 0.68 us
    all_to_all x2 -> x0, waiting for transfers between devices: 227 us -> none  [the longest x1 218 us: local(): lax.all_to_all(rows_all, ('dp', 'expert'), split_axis=0, concat_axis=0, t...]
    pallas_call x0 -> x1, Pallas kernels: none -> 182 us  [local(): pl.pallas_call(kernel, out_shape=(sds((FF, D), BF), sds((SEC, D), BF), sd...]
    psum x1 -> x0, waiting for transfers between devices: 107 us -> none  [local(): total = lax.psum(sectioned.astype(jnp.bfloat16), 'expert')]
    all_gather x1 -> x0, waiting for transfers between devices: 95.7 us -> none  [local(): lax.all_gather(proj_weight, 'dp', axis=0, tiled=True)]
    reduce_scatter x1 -> x0, waiting for transfers between devices: 50.7 us -> none  [local(): lax.psum_scatter(lax.dot_general(attn_out, resid_grad, (((0,), (0,)), (()...]
    dot_general x5 -> x1, matrix products: 47.8 us -> 2.87 us  [dot(): lax.dot_general(a, b, (((ca,), (cb,)), ((), ())), preferred_element_type=...]
    reshape x5 -> x0, local copies, waits for them, and re-layouts: 44.2 us -> none  [the longest x1 22.9 us: local(): scaled = (recv_gate[:, :, None] * recv_rows).reshape(n_source * cap, width)]
    all_to_all x2 -> x0, starting transfers between devices: 35.1 us -> none  [the longest x1 23.2 us: local(): lax.all_to_all(partial_grad, ('dp', 'expert'), split_axis=0, concat_axis=...]
  transfers between devices with their start and end apart: 5 -> 0, of which waited for: 5 -> 0; matrix products, arithmetic and copies ran while one was open for 12% -> 0% of each run, Pallas kernels for 0% -> 0%
where the time goes in v2:
time: 195 us; the launch traced here: 194 us
  Pallas kernels  182 us (93%)
  local copies, waits for them, and re-layouts  8.64 us (4%)
  matrix products  2.87 us (1%)
    pallas_call x1, Pallas kernels, local(): pl.pallas_call(kernel, out_shape=(sds((FF, D), BF), sds((SEC, D), BF), sd...  182 us
    unnamed x10, local copies, waits for them, and re-layouts  8.64 us

profile of v2, /device:TPU:1, one launch (start us, length us, event | category | flops | bytes accessed | tf_op | source)
XLA Modules:
  0.0 194.1 jit_solution(14388868959319512788)
XLA Ops:
  0.6 0.0 copy-start.1
  0.6 181.9 %layer_backward.1 = (bf16[720,2880]{1,0:T(8,128)(2,1)}, bf16[512,2880]{1,0:T(8,128)(2,1)}, bf16[7,2560,256]{2,1,0:T(8,128)(2,1)}, bf16[4,4,4,160,256]{4,3,2,1,0:...) custom-call(bf16[2880,128]{1,0:T(8,128)(2,1)} %bitcast.18, s32[4,128]{1,0:T(4,128)} %bitcast.19, ...), custom_call_target="tpu_custom_call" | custom-call | flops 49999998976 | bytes 400000000 | tf_op jit(solution)/shard_map/layer_backward/pallas_call | solution.py:827
  182.5 0.0 copy-done.1
  182.5 2.9 %add_convert_fusion = bf16[512,2880]{1,0:T(8,128)(2,1)S(1)} fusion(bf16[512,2880]{1,0:T(8,128)(2,1)} %get-tuple-element.10, bf16[2880,32]{0,1:T(8,128)(2,1)S(1)} %copy-done.1, f32[32,512]{1,0:T(8,128)} %get-tuple-element.11), kind=kOutput, calls=%fused_computation | convolution fusion | flops 98811904 | bytes 6148096 | tf_op jit(solution)/shard_map/dot_general | solution.py:61
  185.4 0.0 copy-start
  185.4 2.7 %copy.13 = bf16[512,2880]{0,1:T(8,128)(2,1)} copy(bf16[512,2880]{1,0:T(8,128)(2,1)S(1)} %add_convert_fusion) | data formatting | bytes 5898240
  188.2 0.0 copy-done
  188.2 0.8 copy.18
  189.0 0.0 copy-start.2
  189.0 4.5 %copy.19 = bf16[1,720,2880]{2,1,0:T(8,128)(2,1)} copy(bf16[1,720,2880]{2,1,0:T(8,128)(2,1)} %bitcast.12) | data formatting | bytes 8294400
  193.5 0.0 copy-done.2
  193.5 0.6 copy.20
Async XLA Ops:
  0.6 181.9 %copy-start.1 = (bf16[2880,32]{0,1:T(8,128)(2,1)S(1)}, bf16[2880,32]{0,1:T(8,128)(2,1)}, u32[]{:S(2)}) copy-start(bf16[2880,32]{0,1:T(8,128)(2,1)} %param.11) | copy-start | bytes 552964
  185.4 2.7 %copy-start = (bf16[128,2048]{1,0:T(8,128)(2,1)S(1)}, bf16[128,2048]{1,0:T(8,128)(2,1)}, u32[]{:S(2)}) copy-start(bf16[128,2048]{1,0:T(8,128)(2,1)} %get-tuple-element.22) | copy-start | bytes 1572868
  189.0 4.5 %copy-start.2 = (f32[4,128]{1,0:T(4,128)S(1)}, f32[4,128]{1,0:T(4,128)}, u32[]{:S(2)}) copy-start(f32[4,128]{1,0:T(4,128)} %get-tuple-element.13) | copy-start | bytes 6148

commit v3 on v2

--- a/solution.py
+++ b/solution.py
@@ -20,39 +20,39 @@
 SEC = 512
 HID = 2048
 CH = 256
-NA = 7
-NC = 4
+NA = 8
+NC = 3
 CB = NA * CH
-STEPS = 28
+STEPS = 29
 AT = {
-    "gate_hidden": (18,),
-    "tail_core": (10,),
-    "a_core": (2, 3, 4, 7, 8, 13, 14),
-    "a_work": (21, 22, 23, 24, 25, 26, 27),
-    "send_sections": (4,),
+    "a_send_z": (0, 1, 2, 3, 5, 6, 8, 9),
+    "pick_own": (3,),
     "attn_part": (17,),
-    "known_part": (14,),
-    "tail_pick": (11,),
-    "a_send_z": (0, 1, 2, 4, 5, 7, 8),
-    "tail_z": (5,),
-    "tok_c_ring": (2,),
-    "tok_a_send": (2,),
-    "y_send": (7, 8, 9, 10, 11, 19, 20),
-    "c_work": (20, 21, 24, 27),
-    "c_core": (12, 15, 18, 24),
-    "sum_core": (17,),
+    "tok_a_send": (1,),
+    "sum_x": (24,),
+    "c_core": (15, 19, 23),
     "pack_hidden": (1,),
-    "c_pick": (13, 17, 20, 25),
+    "tok_c_ring": (1,),
+    "send_sections": (5,),
+    "c_send_z": (7, 15, 19),
+    "y_send": (6, 7, 10, 12, 13, 14, 19, 20),
+    "sum_z": (21,),
+    "a_pick": (3, 4, 6, 9, 10, 11, 17, 18),
+    "c_work": (21, 23, 28),
+    "tail_pick": (14,),
+    "sum_core": (15,),
+    "tail_core": (11,),
+    "c_pick": (18, 20, 24),
+    "tail_z": (6,),
+    "tok_a_ring": (5,),
+    "tail_own_core": (1,),
+    "a_core": (1, 2, 4, 5, 7, 8, 15, 16),
+    "gate_hidden": (19,),
+    "known_part": (11,),
+    "y_ring": (11, 14, 16, 18, 19, 20, 23, 25),
     "give_z": (25,),
-    "give_core": (27,),
-    "y_ring": (11, 15, 16, 17, 18, 24, 25),
-    "sum_x": (24,),
-    "c_send_z": (5, 12, 16, 18),
-    "sum_z": (22,),
-    "tok_a_ring": (8,),
-    "pick_own": (2,),
-    "tail_own_core": (1,),
-    "a_pick": (2, 5, 6, 7, 8, 13, 14),
+    "a_work": (20, 21, 22, 24, 25, 26, 27, 28),
+    "give_core": (28,),
 }
 ROWS = 2560
 
@@ -112,12 +112,17 @@
     return jnp.where(iota((n, n), 0) == iota((n, n), 1), 1.0, 0.0).astype(BF)
 
 
+def four(ref):
+    part = [ref[i].astype(F32) for i in range(4)]
+    return ((part[0] + part[1]) + (part[2] + part[3])).astype(BF)
+
+
 def kernel(
     og_h, ids_h, log_h, ao, pw_h, rw_h, hid_h, w_h,
     dg, total, ra, rc, attn, lg, qt,
     og, ids, logits, pw, rw, hp, yt, za, zc, zs, sb, sa, sc, sss, rsd, rbuf, w, hid, hgt, acc,
     stg, stl, aos, aot, ms, mr, rpo, rpt, s1, cb, zb_, p1, xb_, xg,
-    vs, yr, xr, zr, cr, rr, q0, q1, q2, q3,
+    vs, yr, xr, cr, rr, q0, q3,
     a_s, a_r, c_s, c_r, k_s, k_r, g_s, g_r, t_s, t_r, ls,
 ):
     y, x, z, c = place()
@@ -126,6 +131,8 @@
     xp = [dev(y, x + i, z, c) for i in (1, 2, 3)]
     yp = [dev(y + i, x, z, c) for i in (1, 2, 3)]
     cp = dev(y, x, z, 1 - c)
+    yxp = [dev(y + n // 4, x + n % 4, z, c) for n in range(16)]
+    zcp = [dev(y, x, z + m // 2, lax.rem(c + m % 2, 2)) for m in range(8)]
     loads = [
         pltpu.make_async_copy(a, b, ls.at[5 + n])
         for n, (a, b) in enumerate(
@@ -142,14 +149,14 @@
         l.start()
     load_hid(0).start()
     load_hid(1).start()
-    greet(zp + xp + yp + [cp])
+    greet(yxp[1:] + zcp[1:])
     for l in loads[:3]:
         l.wait()
     dense, pos = dense_gates(ids, logits)
     side = [og[MAIN:D, :], pos.astype(BF), dense.astype(BF)]
     yt[0, :, MAIN:DP] = dot(eye(TOK), jnp.concatenate(side, axis=0), 1, 1).astype(BF)
 
-    @pl.loop(0, MAIN // CH)
+    @pl.loop(NA, NA + NC)
     def _(k):
         rows = pl.ds(pl.multiple_of(k * CH, CH), CH)
         yt[0, :, rows] = dot(eye(TOK), og[rows, :], 1, 1).astype(BF)
@@ -349,55 +356,23 @@
     for i in range(2):
         tok(0, i).start()
 
-    def gate_hidden(_):
-        s_xown().wait()
-        for i in range(3):
-            s_x(i).wait_recv()
-        rows = rsd[...].reshape(ROWS, 128)
-        sel = jnp.where(iota((8, 128), 1) == 96 + e, 1.0, 0.0).astype(BF)
-        gate = dot(sel, rows, 1, 1)[0:1, :]
-
-        @pl.loop(0, FF // 16)
-        def _(b):
-            rb = pl.ds(pl.multiple_of(b * 16, 16), 16)
-            hgt[rb, :] = (hgt[rb, :].astype(F32) * gate).astype(BF)
-
-        stl[...] = dot(hgt[...], rows, 1, 0)[:, 0:64].astype(BF)
-        put_tail().start()
-        @pl.loop(0, 4)
-        def _(b):
-            rb = pl.ds(pl.multiple_of(b * 640, 640), 640)
-            g = dot(hidden(b), w[:, MAIN:D], 1, 0)
-            part = rsd[b].reshape(640, 128)[:, 0:64].astype(F32)
-            acc[rb, :] = jnp.concatenate([g * part, jnp.zeros((640, 64), F32)], axis=1)
-
-    def tail_core(_):
-        for i in range(3):
-            s_z(1, i).wait_recv()
-            s_c(1, i).start()
-
-    def a_core(k):
-        for i in range(3):
-            a_z(k, i).wait_recv()
-            a_c(k, i).start()
-
-    def a_work(k):
-        for i in range(2):
-            a_f(k, i).wait_recv()
-        fetch = pltpu.make_async_copy(ra.at[k], rbuf.at[0], ls.at[3])
-        fetch.start()
-
-        @pl.when(k > 0)
-        def _():
-            put(0, k - 1).wait()
-
-        fetch.wait()
-        work(0, k)
-
-    def send_sections(_):
-        for i in range(3):
-            sections(i).start()
-        own_section().start()
+    @pl.loop(0, NA)
+    def _(k):
+        rows = pl.ds(pl.multiple_of(k * CH, CH), CH)
+        yt[0, :, rows] = dot(eye(TOK), og[rows, :], 1, 1).astype(BF)
+
+
+    def a_send_z(k):
+        for i in range(4):
+            a_z(k, i).start()
+        a_own(k).start()
+
+    def pick_own(_):
+        s_own(0).wait()
+        s_z(0, 3).wait_recv()
+        for i in range(3):
+            s_c(0, i).wait_recv()
+        picks(0)
 
     def attn_part(_):
         @pl.loop(0, 4)
@@ -409,65 +384,67 @@
             back(i).start()
         mr[y] = ms[3]
 
-    def known_part(_):
+    def tok_a_send(_):
         for i in range(2):
-            tok_f(1, i).wait_recv()
-        own_section().wait()
-        for i in range(3):
-            sections(i).wait_recv()
-        unit = eye(SEC)
-        for i in range(4):
-            aot[:, i * TOK : (i + 1) * TOK] = dot(unit, aos[i], 1, 1).astype(BF)
-
-        @pl.loop(0, MAIN // CH)
-        def _(k):
-            block = yt[:, :, cols_of(k)].reshape(4 * TOK, CH)
-            s1[:, cols_of(k)] = dot(aot[...], block, 1, 0).astype(BF)
-
-        last = yt[:, :, MAIN:DP].reshape(4 * TOK, 128)
-        s1[:, MAIN:D] = dot(aot[...], last, 1, 0)[:, 0:64].astype(BF)
-        g_core().start()
-
-    def tail_pick(_):
-        s_own(1).wait()
-        s_z(1, 3).wait_recv()
-        for i in range(3):
-            s_c(1, i).wait_recv()
-
-        @pl.loop(1, 4)
-        def _(i):
-            picks(i)
+            tok(1, i).start()
+
+    def sum_x(_):
+        for i in range(3):
+            g_x(i).wait_recv()
+        rows = pl.ds(pl.multiple_of(x * 16, 16), 16)
+        add = p1[rows, :].astype(F32) + xb_[0].astype(F32)
+        xg[rows, :] = (add + (xb_[1].astype(F32) + xb_[2].astype(F32))).astype(BF)
+        for i in range(3):
+            h_x(i).start()
+
+    def c_core(j):
+        for i in range(3):
+            c_z(j, i).wait_recv()
+            c_c(j, i).start()
+
+    def pack_hidden(_):
+        @pl.loop(0, CAP // 2)
+        def _(b):
+            load_hid(b).wait()
+            two = [
+                dot(eye(TOK), hp[lax.rem(b, 2), h], 1, 1).reshape(16, 8, FF) for h in range(2)
+            ]
+            rows = pl.ds(pl.multiple_of(b * 16, 16), 16)
+            hid[:, rows, :] = jnp.concatenate(two, axis=1).astype(BF)
+
+            @pl.when(b < CAP // 2 - 2)
+            def _():
+                load_hid(b + 2).start()
+
+        unit = eye(FF)
 
         @pl.loop(0, 4)
-        def _(i):
-            got = dot(sb[i], zs[i], 1, 0).astype(BF)
-            for xx in range(4):
-                sss[xx, lax.rem(y + i, 4)] = got[xx * 160 : (xx + 1) * 160]
-
-        for i in range(3):
-            s_x(i).start()
-        s_xown().start()
-
-    def a_send_z(k):
-        for i in range(4):
-            a_z(k, i).start()
-        a_own(k).start()
-
-    def tail_z(_):
-        for i in range(2):
-            tok_f(0, i).wait_recv()
-        for i in range(4):
-            s_z(1, i).start()
-        s_own(1).start()
+        def _(b):
+            rb = pl.ds(pl.multiple_of(b * 640, 640), 640)
+            hgt[:, rb] = dot(unit, hidden(b), 1, 1).astype(BF)
+
+        loads[3].wait()
+        loads[4].wait()
+        loads[5].wait()
+        rpo[...] = dot(rw[...], pw[...], 1, 0).astype(BF)
+        for i in range(3):
+            rp(i).start()
+        rpt[y] = rpo[...]
 
     def tok_c_ring(_):
         for i in range(2):
             tok(0, i).wait_recv()
             tok_f(0, i).start()
 
-    def tok_a_send(_):
-        for i in range(2):
-            tok(1, i).start()
+    def send_sections(_):
+        for i in range(3):
+            sections(i).start()
+        own_section().start()
+
+    def c_send_z(j):
+        for i in range(4):
+            c_z(j, i).start()
+        c_own(j).start()
 
     def y_send(k):
         a_xown(k).wait()
@@ -475,6 +452,26 @@
             a_x(k, i).wait_recv()
         for i in range(2):
             a_y(k, i).start()
+
+    def sum_z(_):
+        for i in range(3):
+            g_z(i).wait_recv()
+        add = s1[at_z, :].astype(F32) + zb_[0].astype(F32)
+        p1[...] = (add + (zb_[1].astype(F32) + zb_[2].astype(F32))).astype(BF)
+        for i in range(3):
+            g_x(i).start()
+
+    def a_pick(k):
+        a_own(k).wait()
+        a_z(k, 3).wait_recv()
+        for i in range(3):
+            a_c(k, i).wait_recv()
+        got = dot(sb[0], za[k], 1, 0).astype(BF)
+        for xx in range(4):
+            sa[k, xx] = got[xx * 160 : (xx + 1) * 160]
+        for i in range(3):
+            a_x(k, i).start()
+        a_xown(k).start()
 
     def c_work(j):
         c_xown(j).wait()
@@ -498,10 +495,25 @@
             f.wait()
         work(1, NA + j)
 
-    def c_core(j):
-        for i in range(3):
-            c_z(j, i).wait_recv()
-            c_c(j, i).start()
+    def tail_pick(_):
+        s_own(1).wait()
+        s_z(1, 3).wait_recv()
+        for i in range(3):
+            s_c(1, i).wait_recv()
+
+        @pl.loop(1, 4)
+        def _(i):
+            picks(i)
+
+        @pl.loop(0, 4)
+        def _(i):
+            got = dot(sb[i], zs[i], 1, 0).astype(BF)
+            for xx in range(4):
+                sss[xx, lax.rem(y + i, 4)] = got[xx * 160 : (xx + 1) * 160]
+
+        for i in range(3):
+            s_x(i).start()
+        s_xown().start()
 
     def sum_core(_):
         g_core().wait()
@@ -515,34 +527,10 @@
         for i in range(3):
             g_z(i).start()
 
-    def pack_hidden(_):
-        @pl.loop(0, CAP // 2)
-        def _(b):
-            load_hid(b).wait()
-            two = [
-                dot(eye(TOK), hp[lax.rem(b, 2), h], 1, 1).reshape(16, 8, FF) for h in range(2)
-            ]
-            rows = pl.ds(pl.multiple_of(b * 16, 16), 16)
-            hid[:, rows, :] = jnp.concatenate(two, axis=1).astype(BF)
-
-            @pl.when(b < CAP // 2 - 2)
-            def _():
-                load_hid(b + 2).start()
-
-        unit = eye(FF)
-
-        @pl.loop(0, 4)
-        def _(b):
-            rb = pl.ds(pl.multiple_of(b * 640, 640), 640)
-            hgt[:, rb] = dot(unit, hidden(b), 1, 1).astype(BF)
-
-        loads[3].wait()
-        loads[4].wait()
-        loads[5].wait()
-        rpo[...] = dot(rw[...], pw[...], 1, 0).astype(BF)
-        for i in range(3):
-            rp(i).start()
-        rpt[y] = rpo[...]
+    def tail_core(_):
+        for i in range(3):
+            s_z(1, i).wait_recv()
+            s_c(1, i).start()
 
     def c_pick(j):
         c_own(j).wait()
@@ -565,104 +553,129 @@
             c_x(j, i).start()
         c_xown(j).start()
 
-    def give_z(_):
-        for i in range(3):
-            h_x(i).wait_recv()
-        for i in range(3):
-            h_z(i).start()
-        h_own().start()
-
-    def give_core(_):
-        for i in range(3):
-            h_z(i).wait_recv()
-        h_own().wait()
-        h_core().start()
+    def tail_z(_):
+        for i in range(2):
+            tok_f(0, i).wait_recv()
+        for i in range(4):
+            s_z(1, i).start()
+        s_own(1).start()
+
+    def tok_a_ring(_):
+        for i in range(2):
+            tok(1, i).wait_recv()
+            tok_f(1, i).start()
+
+    def tail_own_core(_):
+        for i in range(3):
+            s_z(0, i).wait_recv()
+            s_c(0, i).start()
+
+    def a_core(k):
+        for i in range(3):
+            a_z(k, i).wait_recv()
+            a_c(k, i).start()
+
+    def gate_hidden(_):
+        s_xown().wait()
+        for i in range(3):
+            s_x(i).wait_recv()
+        rows = rsd[...].reshape(ROWS, 128)
+        sel = jnp.where(iota((8, 128), 1) == 96 + e, 1.0, 0.0).astype(BF)
+        gate = dot(sel, rows, 1, 1)[0:1, :]
+
+        @pl.loop(0, FF // 16)
+        def _(b):
+            rb = pl.ds(pl.multiple_of(b * 16, 16), 16)
+            hgt[rb, :] = (hgt[rb, :].astype(F32) * gate).astype(BF)
+
+        stl[...] = dot(hgt[...], rows, 1, 0)[:, 0:64].astype(BF)
+        put_tail().start()
+        @pl.loop(0, 4)
+        def _(b):
+            rb = pl.ds(pl.multiple_of(b * 640, 640), 640)
+            g = dot(hidden(b), w[:, MAIN:D], 1, 0)
+            part = rsd[b].reshape(640, 128)[:, 0:64].astype(F32)
+            acc[rb, :] = jnp.concatenate([g * part, jnp.zeros((640, 64), F32)], axis=1)
+
+    def known_part(_):
+        for i in range(2):
+            tok_f(1, i).wait_recv()
+        own_section().wait()
+        for i in range(3):
+            sections(i).wait_recv()
+        unit = eye(SEC)
+        for i in range(4):
+            aot[:, i * TOK : (i + 1) * TOK] = dot(unit, aos[i], 1, 1).astype(BF)
+
+        @pl.loop(0, MAIN // CH)
+        def _(k):
+            block = yt[:, :, cols_of(k)].reshape(4 * TOK, CH)
+            s1[:, cols_of(k)] = dot(aot[...], block, 1, 0).astype(BF)
+
+        last = yt[:, :, MAIN:DP].reshape(4 * TOK, 128)
+        s1[:, MAIN:D] = dot(aot[...], last, 1, 0)[:, 0:64].astype(BF)
+        g_core().start()
 
     def y_ring(k):
         for i in range(2):
             a_y(k, i).wait_recv()
             a_f(k, i).start()
 
-    def sum_x(_):
-        for i in range(3):
-            g_x(i).wait_recv()
-        rows = pl.ds(pl.multiple_of(x * 16, 16), 16)
-        add = p1[rows, :].astype(F32) + xb_[0].astype(F32)
-        xg[rows, :] = (add + (xb_[1].astype(F32) + xb_[2].astype(F32))).astype(BF)
-        for i in range(3):
-            h_x(i).start()
-
-    def c_send_z(j):
-        for i in range(4):
-            c_z(j, i).start()
-        c_own(j).start()
-
-    def sum_z(_):
-        for i in range(3):
-            g_z(i).wait_recv()
-        add = s1[at_z, :].astype(F32) + zb_[0].astype(F32)
-        p1[...] = (add + (zb_[1].astype(F32) + zb_[2].astype(F32))).astype(BF)
-        for i in range(3):
-            g_x(i).start()
-
-    def tok_a_ring(_):
+    def give_z(_):
+        for i in range(3):
+            h_x(i).wait_recv()
+        for i in range(3):
+            h_z(i).start()
+        h_own().start()
+
+    def a_work(k):
         for i in range(2):
-            tok(1, i).wait_recv()
-            tok_f(1, i).start()
-
-    def pick_own(_):
-        s_own(0).wait()
-        s_z(0, 3).wait_recv()
-        for i in range(3):
-            s_c(0, i).wait_recv()
-        picks(0)
-
-    def tail_own_core(_):
-        for i in range(3):
-            s_z(0, i).wait_recv()
-            s_c(0, i).start()
-
-    def a_pick(k):
-        a_own(k).wait()
-        a_z(k, 3).wait_recv()
-        for i in range(3):
-            a_c(k, i).wait_recv()
-        got = dot(sb[0], za[k], 1, 0).astype(BF)
-        for xx in range(4):
-            sa[k, xx] = got[xx * 160 : (xx + 1) * 160]
-        for i in range(3):
-            a_x(k, i).start()
-        a_xown(k).start()
+            a_f(k, i).wait_recv()
+        fetch = pltpu.make_async_copy(ra.at[k], rbuf.at[0], ls.at[3])
+        fetch.start()
+
+        @pl.when(k > 0)
+        def _():
+            put(0, k - 1).wait()
+
+        fetch.wait()
+        work(0, k)
+
+    def give_core(_):
+        for i in range(3):
+            h_z(i).wait_recv()
+        h_own().wait()
+        h_core().start()
 
     parts = {
+        "a_send_z": a_send_z,
+        "pick_own": pick_own,
+        "attn_part": attn_part,
+        "tok_a_send": tok_a_send,
+        "sum_x": sum_x,
+        "c_core": c_core,
+        "pack_hidden": pack_hidden,
+        "tok_c_ring": tok_c_ring,
+        "send_sections": send_sections,
+        "c_send_z": c_send_z,
+        "y_send": y_send,
+        "sum_z": sum_z,
+        "a_pick": a_pick,
+        "c_work": c_work,
+        "tail_pick": tail_pick,
+        "sum_core": sum_core,
+        "tail_core": tail_core,
+        "c_pick": c_pick,
+        "tail_z": tail_z,
+        "tok_a_ring": tok_a_ring,
+        "tail_own_core": tail_own_core,
+        "a_core": a_core,
         "gate_hidden": gate_hidden,
-        "tail_core": tail_core,
-        "a_core": a_core,
+        "known_part": known_part,
+        "y_ring": y_ring,
+        "give_z": give_z,
         "a_work": a_work,
-        "send_sections": send_sections,
-        "attn_part": attn_part,
-        "known_part": known_part,
-        "tail_pick": tail_pick,
-        "a_send_z": a_send_z,
-        "tail_z": tail_z,
-        "tok_c_ring": tok_c_ring,
-        "tok_a_send": tok_a_send,
-        "y_send": y_send,
-        "c_work": c_work,
-        "c_core": c_core,
-        "sum_core": sum_core,
-        "pack_hidden": pack_hidden,
-        "c_pick": c_pick,
-        "give_z": give_z,
         "give_core": give_core,
-        "y_ring": y_ring,
-        "sum_x": sum_x,
-        "c_send_z": c_send_z,
-        "sum_z": sum_z,
-        "tok_a_ring": tok_a_ring,
-        "pick_own": pick_own,
-        "tail_own_core": tail_own_core,
-        "a_pick": a_pick,
     }
 
     @pl.loop(0, STEPS)
@@ -678,58 +691,40 @@
             def _(part=parts[key], number=number):
                 part(number)
 
-    exact = lax.Precision.HIGHEST
-    at_slot = iota((160, 128), 1) == lax.shift_right_logical(iota((160, 128), 0), 3)
-    fold = jnp.where((iota((8, 160), 1) & 7) == iota((8, 160), 0), 1.0, 0.0)
-    for b in range(16):
-        sums = jnp.sum(acc[b * 160 : (b + 1) * 160, :], axis=1, keepdims=True)
-        vs[b // 4, b % 4] = dot(fold, jnp.where(at_slot, sums, 0.0), 1, 0, exact)
-
-    def v_y(i):
-        return remote(
-            vs.at[lax.rem(y + i + 1, 4)], yr.at[i], t_s.at[i], t_r.at[i], yp[i]
-        )
-
-    def v_x(i):
-        to = lax.rem(x + i + 1, 4)
-        return remote(vs.at[0, to], xr.at[x], t_s.at[3 + i], t_r.at[3 + i], xp[i])
-
-    def v_z(i):
-        return remote(xr, zr.at[:, z], t_s.at[6 + i], t_r.at[6 + i], zp[i])
-
-    def v_c():
-        return remote(zr, cr.at[:, :, c], t_s.at[9], t_r.at[9], cp)
+    at_slot = iota((4, CAP, 8, 128), 3) == iota((4, CAP, 8, 128), 1)
+    for b in range(4):
+        block = acc[b * 640 : (b + 1) * 640, :].reshape(4, CAP, 8, 128)
+        sums = jnp.sum(block, axis=3, keepdims=True)
+        vs[b] = jnp.sum(jnp.where(at_slot, sums, 0.0), axis=1)
+
+    def v_yx(n):
+        block = vs.at[lax.rem(y + n // 4, 4), lax.rem(x + n % 4, 4)]
+        return remote(block, yr.at[n], t_s.at[n], t_r.at[n], yxp[n])
+
+    def v_zc(m):
+        return remote(xr, cr.at[:, z, c], t_s.at[16 + m], t_r.at[16 + m], zcp[m])
 
     def r_y(i):
-        return remote(rr.at[0], rr.at[3 - i], t_s.at[10 + i], t_r.at[10 + i], yp[i])
-
-    def q_c():
-        return remote(q0, q1, t_s.at[13], t_r.at[13], cp)
-
-    def q_z(i):
-        return remote(q2.at[0], q2.at[1 + i], t_s.at[14 + i], t_r.at[14 + i], zp[i])
+        return remote(rr.at[0], rr.at[3 - i], t_s.at[24 + i], t_r.at[24 + i], yp[i])
+
+    def q_zc(m):
+        return remote(q0.at[0], q0.at[m], t_s.at[27 + m], t_r.at[27 + m], zcp[m])
 
     def q_x(i):
-        return remote(q3.at[0], q3.at[1 + i], t_s.at[17 + i], t_r.at[17 + i], xp[i])
-
-    for i in range(3):
-        v_y(i).start()
-    for i in range(3):
-        v_y(i).wait()
-    vs[0] = vs[y] + yr[0] + yr[1] + yr[2]
-    for i in range(3):
-        v_x(i).start()
-    xr[x] = vs[0, x]
-    for i in range(3):
-        v_x(i).wait()
-    for i in range(3):
-        v_z(i).start()
-    zr[:, z] = xr[...]
-    for i in range(3):
-        v_z(i).wait()
-    v_c().start()
-    cr[:, :, c] = zr[...]
-    v_c().wait()
+        return remote(q3.at[0], q3.at[1 + i], t_s.at[35 + i], t_r.at[35 + i], xp[i])
+
+    for n in range(1, 16):
+        v_yx(n).start()
+    yr[0] = vs[y, x]
+    for n in range(1, 16):
+        v_yx(n).wait()
+    for n in range(4):
+        xr[lax.rem(x + 4 - n, 4)] = (yr[n] + yr[4 + n]) + (yr[8 + n] + yr[12 + n])
+    for m in range(1, 8):
+        v_zc(m).start()
+    cr[:, z, c] = xr[...]
+    for m in range(1, 8):
+        v_zc(m).wait()
     got = cr[...].reshape(NE, 8, 128)
     got = jnp.sum(jnp.where(iota((NE, 8, 128), 1) == z * 2 + c, got, 0.0), axis=1)
     grad = jnp.zeros((NE, TOK), F32)
@@ -750,26 +745,26 @@
     q = jnp.zeros((NE, SEC), F32)
     for t in range(4):
         q = q + dot(rr[t], aos[t], 1, 0)
-    q0[...] = q
-    q_c().start()
+    q0[0] = q.astype(BF)
+    for m in range(1, 8):
+        q_zc(m).start()
     for i in range(3):
         rp(i).wait()
         back(i).wait()
     for t in range(4):
         more = dot(rrow, rpt[t], 0, 0)
         attn[:, t * SEC : (t + 1) * SEC] = (mr[t].astype(F32) + more).astype(BF)
-    q_c().wait()
-    q2[0] = q0[...] + q1[...]
-    for i in range(3):
-        q_z(i).start()
-    for i in range(3):
-        q_z(i).wait()
-    q3[0] = (q2[0] + q2[1]) + (q2[2] + q2[3])
+    for m in range(1, 8):
+        q_zc(m).wait()
+    eight = [q0[m].astype(F32) for m in range(8)]
+    while len(eight) > 1:
+        eight = [eight[m] + eight[m + 1] for m in range(0, len(eight), 2)]
+    q3[0] = eight[0].astype(BF)
     for i in range(3):
         q_x(i).start()
     for i in range(3):
         q_x(i).wait()
-    qt[...] = (q3[0] + q3[1]) + (q3[2] + q3[3])
+    qt[...] = four(q3)
 
     put(0, NA - 1).wait()
     put(1, NA + NC - 1).wait()
@@ -829,7 +824,7 @@
         out_shape=(
             sds((FF, D), BF), sds((SEC, D), BF), sds((NA, ROWS, CH), BF),
             sds((NC, 4, 4, 160, CH), BF), sds((TOK, HID), BF), sds((4, TOK), F32),
-            sds((NE, SEC), F32),
+            sds((NE, SEC), BF),
         ),
         in_specs=[hbm] * 8,
         out_specs=(hbm, hbm, hbm, hbm, vm, vm, vm),
@@ -844,11 +839,11 @@
             v((4, TOK, SEC), BF), v((SEC, SEC), BF), v((4, TOK, SEC), BF), v((4, TOK, SEC), BF),
             v((NE, SEC), BF), v((4, NE, SEC), BF), v((SEC, D), BF), v((256, D), BF),
             v((3, 64, D), BF), v((64, D), BF), v((3, 16, D), BF), v((64, D), BF),
-            v((4, 4, 8, 128), F32), v((3, 4, 8, 128), F32), v((4, 8, 128), F32),
-            v((4, 4, 8, 128), F32), v((4, 4, 2, 8, 128), F32), v((4, NE, TOK), BF),
-            v((NE, SEC), F32), v((NE, SEC), F32), v((4, NE, SEC), F32), v((4, NE, SEC), F32),
+            v((4, 4, 8, 128), F32), v((16, 8, 128), F32), v((4, 8, 128), F32),
+            v((4, 4, 2, 8, 128), F32), v((4, NE, TOK), BF),
+            v((8, NE, SEC), BF), v((4, NE, SEC), BF),
             sem((NA, 16)), sem((NA, 16)), sem((NC + 2, 16)), sem((NC + 2, 16)),
-            sem((17,)), sem((17,)), sem((15,)), sem((15,)), sem((20,)), sem((20,)), sem((32,)),
+            sem((17,)), sem((17,)), sem((15,)), sem((15,)), sem((40,)), sem((40,)), sem((32,)),
         ],
         compiler_params=pltpu.CompilerParams(
             collective_id=0, has_side_effects=True, vmem_limit_bytes=62 * 2**20
@@ -861,7 +856,7 @@
         out_grad.T, expert_ids.T, chosen_logits.T, attn_out, proj_weight.T, router_weight.T,
         jnp.transpose(hidden_act[0], (1, 2, 0)), down_weight[0],
     )
-    more = dot(qt.astype(BF), router_weight, 0, 1)
+    more = dot(qt, router_weight, 0, 1)
     proj_grad = (total.astype(F32) + more).astype(BF)
     return attn, proj_grad, dg[None], lg.T
 

time: 195 us -> 187 us (0.959)
  Pallas kernels: 182 us -> 174 us
    pallas_call x1, Pallas kernels: 182 us -> 174 us  [local(): pl.pallas_call(kernel, out_shape=(sds((FF, D), BF), sds((SEC, D), BF), sd...]
where the time goes in v3:
time: 187 us; the launch traced here: 186 us
  Pallas kernels  174 us (93%)
  local copies, waits for them, and re-layouts  8.64 us (5%)
  matrix products  2.84 us (2%)
    pallas_call x1, Pallas kernels, local(): pl.pallas_call(kernel, out_shape=(sds((FF, D), BF), sds((SEC, D), BF), sd...  174 us
    unnamed x10, local copies, waits for them, and re-layouts  8.64 us

profile of v3, /device:TPU:1, one launch (start us, length us, event | category | flops | bytes accessed | tf_op | source)
XLA Modules:
  0.0 185.8 jit_solution(388717636891343801)
XLA Ops:
  0.6 0.0 copy-start.1
  0.6 173.7 %layer_backward.1 = (bf16[720,2880]{1,0:T(8,128)(2,1)}, bf16[512,2880]{1,0:T(8,128)(2,1)}, bf16[8,2560,256]{2,1,0:T(8,128)(2,1)}, bf16[3,4,4,160,256]{4,3,2,1,0:...) custom-call(bf16[2880,128]{1,0:T(8,128)(2,1)} %bitcast.19, ...), custom_call_target="tpu_custom_call" | custom-call | flops 49999998976 | bytes 400000000 | tf_op jit(solution)/shard_map/layer_backward/pallas_call | solution.py:822
  174.3 0.0 copy-done.1
  174.4 2.8 %add_convert_fusion = bf16[512,2880]{1,0:T(8,128)(2,1)S(1)} fusion(bf16[512,2880]{1,0:T(8,128)(2,1)} %get-tuple-element.10, bf16[32,512]{1,0:T(8,128)(2,1)} %get-tuple-element.11, bf16[2880,32]{0,1:T(8,128)(2,1)S(1)} %copy-done.1), kind=kOutput, calls=%fused_computation | convolution fusion | flops 98795520 | bytes 6115328 | tf_op jit(solution)/shard_map/dot_general | solution.py:61
  177.2 0.0 copy-start
  177.2 2.7 %copy.13 = bf16[512,2880]{0,1:T(8,128)(2,1)} copy(bf16[512,2880]{1,0:T(8,128)(2,1)S(1)} %add_convert_fusion) | data formatting | bytes 5898240
  179.9 0.0 copy-done
  179.9 0.8 copy.18
  180.7 0.0 copy-start.2
  180.7 4.5 %copy.19 = bf16[1,720,2880]{2,1,0:T(8,128)(2,1)} copy(bf16[1,720,2880]{2,1,0:T(8,128)(2,1)} %bitcast.13) | data formatting | bytes 8294400
  185.3 0.0 copy-done.2
  185.3 0.6 copy.20
Async XLA Ops:
  0.6 173.7 %copy-start.1 = (bf16[2880,32]{0,1:T(8,128)(2,1)S(1)}, bf16[2880,32]{0,1:T(8,128)(2,1)}, u32[]{:S(2)}) copy-start(bf16[2880,32]{0,1:T(8,128)(2,1)} %param.11) | copy-start | bytes 552964
  177.2 2.7 %copy-start = (bf16[128,2048]{1,0:T(8,128)(2,1)S(1)}, bf16[128,2048]{1,0:T(8,128)(2,1)}, u32[]{:S(2)}) copy-start(bf16[128,2048]{1,0:T(8,128)(2,1)} %get-tuple-element.22) | copy-start | bytes 1572868
  180.7 4.5 %copy-start.2 = (f32[4,128]{1,0:T(4,128)S(1)}, f32[4,128]{1,0:T(4,128)}, u32[]{:S(2)}) copy-start(f32[4,128]{1,0:T(4,128)} %get-tuple-element.13) | copy-start | bytes 6148

commit v4 on v3

--- a/solution.py
+++ b/solution.py
@@ -213,25 +213,22 @@
         part = za.at[k, src_rows(lax.rem(z + 3 - i, 4), c)]
         return remote(part, part, a_s.at[k, 4 + i], a_r.at[k, 4 + i], cp)
 
-    def x_rows(yy, xx):
-        return pl.ds(pl.multiple_of(yy * 640 + xx * 160, 160), 160)
-
     def a_x(k, i):
         to = lax.rem(x + i + 1, 4)
         return remote(
-            sa.at[k, to], ra.at[k, x_rows(y, x)], a_s.at[k, 7 + i], a_r.at[k, 7 + i], xp[i]
+            sa.at[k, to], ra.at[k, y * 4 + x], a_s.at[k, 7 + i], a_r.at[k, 7 + i], xp[i]
         )
 
     def a_xown(k):
-        return pltpu.make_async_copy(sa.at[k, x], ra.at[k, x_rows(y, x)], a_s.at[k, 15])
+        return pltpu.make_async_copy(sa.at[k, x], ra.at[k, y * 4 + x], a_s.at[k, 15])
 
     def a_y(k, i):
-        part = ra.at[k, pl.ds(pl.multiple_of(y * 640, 640), 640)]
+        part = ra.at[k, pl.ds(y * 4, 4)]
         return remote(part, part, a_s.at[k, 10 + i], a_r.at[k, 10 + i], yp[2 * i])
 
     def a_f(k, i):
         src = lax.rem(y + (3 if i == 0 else 1), 4)
-        part = ra.at[k, pl.ds(pl.multiple_of(src * 640 + 320 * i, 320), 320)]
+        part = ra.at[k, pl.ds(src * 4 + 2 * i, 2)]
         return remote(part, part, a_s.at[k, 12 + i], a_r.at[k, 12 + i], yp[2 * i])
 
     def c_z(j, i):
@@ -339,16 +336,27 @@
     def put_tail():
         return pltpu.make_async_copy(stl, dg.at[:, pl.ds(MAIN, 64)], ls.at[2])
 
-    def work(slot, k):
-        stg[slot] = dot(hgt[...], rbuf[slot], 1, 0).astype(BF)
-        put(slot, k).start()
+    def fetch(slot, k, b):
+        src = ra.at[k, pl.ds(b * 4, 4)] if slot == 0 else rc.at[k, b]
+        return pltpu.make_async_copy(src, rbuf.at[slot, pl.ds(b * 4, 4)], ls.at[16 + slot * 4 + b])
+
+    def work(slot, first, n):
+        k = first + n
 
         @pl.loop(0, 4)
         def _(b):
             rb = pl.ds(pl.multiple_of(b * 640, 640), 640)
             g = dot(hidden(b), w[:, cols_of(k)], 1, 0)
-            prod = g * rbuf[slot, rb, :].astype(F32)
+            fetch(slot, n, b).wait()
+            prod = g * rbuf[slot, pl.ds(b * 4, 4)].reshape(640, CH).astype(F32)
             acc[rb, :] += prod[:, 0:128] + prod[:, 128:256]
+
+        @pl.when(n > 0)
+        def _():
+            put(slot, k - 1).wait()
+
+        stg[slot] = dot(hgt[...], rbuf[slot].reshape(ROWS, CH), 1, 0).astype(BF)
+        put(slot, k).start()
 
     for i in range(4):
         s_z(0, i).start()
@@ -477,23 +485,9 @@
         c_xown(j).wait()
         for i in range(3):
             c_x(j, i).wait_recv()
-        fetches = [
-            pltpu.make_async_copy(
-                rc.at[j, yy, xx], rbuf.at[1, pl.ds(yy * 640 + xx * 160, 160)],
-                ls.at[16 + yy * 4 + xx],
-            )
-            for yy in range(4) for xx in range(4)
-        ]
-        for f in fetches:
-            f.start()
-
-        @pl.when(j > 0)
-        def _():
-            put(1, NA + j - 1).wait()
-
-        for f in fetches:
-            f.wait()
-        work(1, NA + j)
+        for b in range(4):
+            fetch(1, j, b).start()
+        work(1, NA, j)
 
     def tail_pick(_):
         s_own(1).wait()
@@ -631,15 +625,9 @@
     def a_work(k):
         for i in range(2):
             a_f(k, i).wait_recv()
-        fetch = pltpu.make_async_copy(ra.at[k], rbuf.at[0], ls.at[3])
-        fetch.start()
-
-        @pl.when(k > 0)
-        def _():
-            put(0, k - 1).wait()
-
-        fetch.wait()
-        work(0, k)
+        for b in range(4):
+            fetch(0, k, b).start()
+        work(0, 0, k)
 
     def give_core(_):
         for i in range(3):
@@ -822,7 +810,7 @@
     dg, total, _, _, attn, lg, qt = pl.pallas_call(
         kernel,
         out_shape=(
-            sds((FF, D), BF), sds((SEC, D), BF), sds((NA, ROWS, CH), BF),
+            sds((FF, D), BF), sds((SEC, D), BF), sds((NA, 16, 160, CH), BF),
             sds((NC, 4, 4, 160, CH), BF), sds((TOK, HID), BF), sds((4, TOK), F32),
             sds((NE, SEC), BF),
         ),
@@ -833,7 +821,7 @@
             v((NE, D), BF), v((2, 2, FF, TOK), BF), v((4, TOK, DP), BF),
             v((NA, 1024, CH), BF), v((NC, 4, 1024, CH), BF), v((4, 1024, 128), BF),
             v((4, 640, 1024), BF), v((NA, 4, 160, CH), BF), v((2, 4, 4, 160, CH), BF),
-            v((4, 4, 160, 128), BF), v((4, 4, 160, 128), BF), v((2, ROWS, CH), BF),
+            v((4, 4, 160, 128), BF), v((4, 4, 160, 128), BF), v((2, 16, 160, CH), BF),
             v((FF, D), BF), v((16, 160, FF), BF), v((FF, ROWS), BF),
             v((ROWS, 128), F32), v((2, FF, CH), BF), v((FF, 64), BF),
             v((4, TOK, SEC), BF), v((SEC, SEC), BF), v((4, TOK, SEC), BF), v((4, TOK, SEC), BF),

time: 187 us -> 184 us (0.984)
  Pallas kernels: 174 us -> 171 us
    pallas_call x1, Pallas kernels: 174 us -> 171 us  [local(): pl.pallas_call(kernel, out_shape=(sds((FF, D), BF), sds((SEC, D), BF), sd...]
where the time goes in v4:
time: 184 us
  Pallas kernels  171 us (93%)
  local copies, waits for them, and re-layouts  8.64 us (5%)
  matrix products  2.84 us (2%)
    pallas_call x1, Pallas kernels, local(): pl.pallas_call(kernel, out_shape=(sds((FF, D), BF), sds((SEC, D), BF), sd...  171 us
    unnamed x10, local copies, waits for them, and re-layouts  8.64 us

profile of v4, /device:TPU:1, one launch (start us, length us, event | category | flops | bytes accessed | tf_op | source)
XLA Modules:
  0.0 183.6 jit_solution(18279885913936304683)
XLA Ops:
  0.6 0.0 copy-start.1
  0.6 171.5 %layer_backward.1 = (bf16[720,2880]{1,0:T(8,128)(2,1)}, bf16[512,2880]{1,0:T(8,128)(2,1)}, bf16[8,16,160,256]{3,2,1,0:T(8,128)(2,1)}, bf16[3,4,4,160,256]{4,3,2,...) custom-call(bf16[2880,128]{1,0:T(8,128)(2,1)} %bitcast.19, ...), custom_call_target="tpu_custom_call" | custom-call | flops 49999998976 | bytes 400000000 | tf_op jit(solution)/shard_map/layer_backward/pallas_call | solution.py:810
  172.1 0.0 copy-done.1
  172.2 2.8 %add_convert_fusion = bf16[512,2880]{1,0:T(8,128)(2,1)S(1)} fusion(bf16[512,2880]{1,0:T(8,128)(2,1)} %get-tuple-element.10, bf16[32,512]{1,0:T(8,128)(2,1)} %get-tuple-element.11, bf16[2880,32]{0,1:T(8,128)(2,1)S(1)} %copy-done.1), kind=kOutput, calls=%fused_computation | convolution fusion | flops 98795520 | bytes 6115328 | tf_op jit(solution)/shard_map/dot_general | solution.py:61
  175.0 0.0 copy-start
  175.0 2.7 %copy.13 = bf16[512,2880]{0,1:T(8,128)(2,1)} copy(bf16[512,2880]{1,0:T(8,128)(2,1)S(1)} %add_convert_fusion) | data formatting | bytes 5898240
  177.7 0.0 copy-done
  177.7 0.8 copy.18
  178.5 0.0 copy-start.2
  178.5 4.5 %copy.19 = bf16[1,720,2880]{2,1,0:T(8,128)(2,1)} copy(bf16[1,720,2880]{2,1,0:T(8,128)(2,1)} %bitcast.13) | data formatting | bytes 8294400
  183.1 0.0 copy-done.2
  183.1 0.6 copy.20
Async XLA Ops:
  0.6 171.5 %copy-start.1 = (bf16[2880,32]{0,1:T(8,128)(2,1)S(1)}, bf16[2880,32]{0,1:T(8,128)(2,1)}, u32[]{:S(2)}) copy-start(bf16[2880,32]{0,1:T(8,128)(2,1)} %param.11) | copy-start | bytes 552964
  175.0 2.7 %copy-start = (bf16[128,2048]{1,0:T(8,128)(2,1)S(1)}, bf16[128,2048]{1,0:T(8,128)(2,1)}, u32[]{:S(2)}) copy-start(bf16[128,2048]{1,0:T(8,128)(2,1)} %get-tuple-element.22) | copy-start | bytes 1572868
  178.5 4.5 %copy-start.2 = (f32[4,128]{1,0:T(4,128)S(1)}, f32[4,128]{1,0:T(4,128)}, u32[]{:S(2)}) copy-start(f32[4,128]{1,0:T(4,128)} %get-tuple-element.13) | copy-start | bytes 6148

commit v5 on v4

--- a/solution.py
+++ b/solution.py
@@ -344,7 +344,8 @@
         k = first + n
 
         @pl.loop(0, 4)
-        def _(b):
+        def _(turn):
+            b = lax.rem(y + 3 + turn, 4)
             rb = pl.ds(pl.multiple_of(b * 640, 640), 640)
             g = dot(hidden(b), w[:, cols_of(k)], 1, 0)
             fetch(slot, n, b).wait()
@@ -623,10 +624,11 @@
         h_own().start()
 
     def a_work(k):
+        for n in (3, 0, 1):
+            fetch(0, k, lax.rem(y + n, 4)).start()
         for i in range(2):
             a_f(k, i).wait_recv()
-        for b in range(4):
-            fetch(0, k, b).start()
+        fetch(0, k, lax.rem(y + 2, 4)).start()
         work(0, 0, k)
 
     def give_core(_):

time: 184 us -> 185 us (level)
  no operation moved by 1% of the time
where the time goes in v5:
time: 185 us; the launch traced here: 184 us
  Pallas kernels  172 us (93%)
  local copies, waits for them, and re-layouts  8.64 us (5%)
  matrix products  2.84 us (2%)
    pallas_call x1, Pallas kernels, local(): pl.pallas_call(kernel, out_shape=(sds((FF, D), BF), sds((SEC, D), BF), sd...  172 us
    unnamed x10, local copies, waits for them, and re-layouts  8.64 us

profile of v5, /device:TPU:1, one launch (start us, length us, event | category | flops | bytes accessed | tf_op | source)
XLA Modules:
  0.0 184.1 jit_solution(16623824091082807859)
XLA Ops:
  0.6 0.0 copy-start.1
  0.6 171.9 %layer_backward.1 = (bf16[720,2880]{1,0:T(8,128)(2,1)}, bf16[512,2880]{1,0:T(8,128)(2,1)}, bf16[8,16,160,256]{3,2,1,0:T(8,128)(2,1)}, bf16[3,4,4,160,256]{4,3,2,...) custom-call(bf16[2880,128]{1,0:T(8,128)(2,1)} %bitcast.19, ...), custom_call_target="tpu_custom_call" | custom-call | flops 49999998976 | bytes 400000000 | tf_op jit(solution)/shard_map/layer_backward/pallas_call | solution.py:812
  172.6 0.0 copy-done.1
  172.6 2.8 %add_convert_fusion = bf16[512,2880]{1,0:T(8,128)(2,1)S(1)} fusion(bf16[512,2880]{1,0:T(8,128)(2,1)} %get-tuple-element.10, bf16[32,512]{1,0:T(8,128)(2,1)} %get-tuple-element.11, bf16[2880,32]{0,1:T(8,128)(2,1)S(1)} %copy-done.1), kind=kOutput, calls=%fused_computation | convolution fusion | flops 98795520 | bytes 6115328 | tf_op jit(solution)/shard_map/dot_general | solution.py:61
  175.4 0.0 copy-start
  175.4 2.7 %copy.13 = bf16[512,2880]{0,1:T(8,128)(2,1)} copy(bf16[512,2880]{1,0:T(8,128)(2,1)S(1)} %add_convert_fusion) | data formatting | bytes 5898240
  178.2 0.0 copy-done
  178.2 0.8 copy.18
  179.0 0.0 copy-start.2
  179.0 4.5 %copy.19 = bf16[1,720,2880]{2,1,0:T(8,128)(2,1)} copy(bf16[1,720,2880]{2,1,0:T(8,128)(2,1)} %bitcast.13) | data formatting | bytes 8294400
  183.5 0.0 copy-done.2
  183.5 0.6 copy.20
Async XLA Ops:
  0.6 171.9 %copy-start.1 = (bf16[2880,32]{0,1:T(8,128)(2,1)S(1)}, bf16[2880,32]{0,1:T(8,128)(2,1)}, u32[]{:S(2)}) copy-start(bf16[2880,32]{0,1:T(8,128)(2,1)} %param.11) | copy-start | bytes 552964
  175.4 2.7 %copy-start = (bf16[128,2048]{1,0:T(8,128)(2,1)S(1)}, bf16[128,2048]{1,0:T(8,128)(2,1)}, u32[]{:S(2)}) copy-start(bf16[128,2048]{1,0:T(8,128)(2,1)} %get-tuple-element.22) | copy-start | bytes 1572868
  179.0 4.5 %copy-start.2 = (f32[4,128]{1,0:T(4,128)S(1)}, f32[4,128]{1,0:T(4,128)}, u32[]{:S(2)}) copy-start(f32[4,128]{1,0:T(4,128)} %get-tuple-element.13) | copy-start | bytes 6148
